TPU v7x, 512 devices: a whole 4x4x16 slice. The times are simulated.
512 devices in a mesh: seq: 64 (over y_lo, z, core), head: 8 (over x, y_hi).
Axes of the slice: x: 4, y: 4 (y_hi: 2, y_lo: 2; y = y_hi * 2 + y_lo), z: 16, core: 2. Of those that a mesh axis runs over, the one named last changes fastest.
Arguments:
- qkv_fine: bfloat16 [64, 4, 4, 64, 3, 768], P('seq', None, None, 'head'), may hold values from -6 to 6
- grad_out: bfloat16 [64, 2, 2, 32, 768], P('seq', None, None, 'head'), may hold values from -24 to 24
- pool_weight: bfloat16 [27, 3, 768], replicated, may hold values from -1.25 to 1.25
- norm_gain: float32 [3, 96], replicated, may hold values from 0.25 to 1.75
Outputs:
- grad_qkv: bfloat16 [64, 4, 4, 64, 3, 768], P('seq', None, None, 'head')
- grad_pool: float32 [27, 3, 768], replicated
- grad_gain: float32 [3, 96], replicated
All inputs are finite; a program needn't handle non-finite values.
Results may differ from a plain program's by a relative error of at most 0.0065.
Values may be sent and summed in bfloat16 or wider, within the bound.
A program may use at most 128 MiB of HBM per device.

v0:
```python
import jax
import jax.numpy as jnp
from jax import lax
from jax.sharding import PartitionSpec as P

HD = 96
ROW_GROUPS = 16


member_strides = ((0, 2), (1, 4), (2, 4))


def from_behind(block, axis, distance):
    devices = range(lax.axis_size(axis))
    route = [(i - distance, i) for i in devices if i - distance in devices]
    return lax.ppermute(block, axis, route)


def for_sending(x):
    return jax.tree.map(lambda a: a.astype(jnp.bfloat16) if a.dtype == jnp.float32 else a, x)


def normalize(values, gain):
    shaped = values.reshape(values.shape[:-1] + (values.shape[-1] // HD, HD))
    centred = shaped - jnp.mean(shaped, -1, keepdims=True)
    spread = jnp.mean(centred * centred, -1, keepdims=True)
    return (centred * lax.rsqrt(spread + 1e-06) * gain).reshape(values.shape)


def tap_sum(padded, kernel, stride, counts):
    targets = [stride * (count + 1) for count in counts]
    trimmed = padded
    trimmed = jnp.pad(
        trimmed,
        [(0, targets[axis_pos] - trimmed.shape[axis_pos]) for axis_pos in range(3)] + [(0, 0)],
    )
    channels = padded.shape[3]
    phases = trimmed.reshape(
        targets[0] // stride,
        stride,
        targets[1] // stride,
        stride,
        targets[2] // stride,
        stride,
        channels,
    )
    phases = phases.transpose(1, 3, 5, 0, 2, 4, 6)
    summed = jnp.zeros((counts[0], counts[1], counts[2], channels), jnp.float32)
    for offset in range(27):
        frame_off, row_off, col_off = (offset // 9, offset // 3 % 3, offset % 3)
        phase_cells = phases[frame_off % stride, row_off % stride, col_off % stride]
        window = lax.slice(
            phase_cells,
            (frame_off // stride, row_off // stride, col_off // stride, 0),
            (
                frame_off // stride + counts[0],
                row_off // stride + counts[1],
                col_off // stride + counts[2],
                channels,
            ),
        )
        summed = summed + window * kernel[offset]
    return summed


def pool_norm(extended, weight, gain):
    results = []
    for member, stride in member_strides:
        padded = extended[:, :, :, member]
        counts = [(extent - 1) // stride for extent in padded.shape[:3]]
        results.append(normalize(tap_sum(padded, weight[:, member], stride, counts), gain[member]))
    return tuple(results)


def extend(block_cells):
    widened = jnp.concatenate([jnp.zeros_like(block_cells[:, :, :1]), block_cells], 2)
    above_rim = from_behind(widened[:, -1:], "seq", 1)
    kept_rows = (lax.axis_index("seq") % ROW_GROUPS != 0).astype(above_rim.dtype)
    widened = jnp.concatenate([above_rim * kept_rows, widened], 1)
    before = from_behind(widened[-1:], "seq", ROW_GROUPS)
    return jnp.concatenate([before, widened], 0).astype(jnp.float32)


def retract(gradients):
    returned = from_behind(gradients[:1].astype(jnp.bfloat16), "seq", -ROW_GROUPS).astype(
        jnp.float32
    )
    inner = gradients[1:]
    inner = jnp.concatenate([inner[:-1], inner[-1:] + returned], 0)
    kept_rows = (lax.axis_index("seq") % ROW_GROUPS != 0).astype(jnp.float32)
    returned = from_behind(for_sending(inner[:, :1] * kept_rows), "seq", -1)
    inner = inner[:, 1:]
    inner = jnp.concatenate([inner[:, :-1], inner[:, -1:] + returned], 1)
    inner = inner[:, :, 1:]
    return inner


def pooled_backward(cells, weight, gain, inner_work):
    normed, pull_back = jax.vjp(pool_norm, extend(cells), weight, gain)
    grad_extended, grad_weight, grad_gain = pull_back(inner_work(normed))
    grad_cells = retract(grad_extended)
    return (grad_cells, grad_weight, grad_gain)


def attend(query_cells, key_cells, value_cells, grad_cells):
    channels = query_cells.shape[-1]
    head_count = channels // HD
    score_scale = HD ** (-0.5)
    queries = query_cells.astype(jnp.bfloat16).reshape(-1, head_count, HD)
    grad_rows = grad_cells.reshape(-1, head_count, HD)
    key_part = key_cells.astype(jnp.bfloat16).reshape(1, -1, channels)
    value_part = value_cells.astype(jnp.bfloat16).reshape(1, -1, channels)
    local_keys = key_part.shape[1]
    key_all, value_all = (
        lax.all_gather(key_part, "seq", axis=0, tiled=True),
        lax.all_gather(value_part, "seq", axis=0, tiled=True),
    )
    key_all = key_all.reshape(-1, head_count, HD)
    value_all = value_all.reshape(-1, head_count, HD)
    scores = (
        jnp.einsum("qhd,khd->hqk", queries, key_all, preferred_element_type=jnp.float32)
        * score_scale
    )
    raised = jnp.exp(scores)
    attention = raised / jnp.sum(raised, -1, keepdims=True)
    attention_low = attention.astype(jnp.bfloat16)
    grad_attention = jnp.einsum(
        "qhd,khd->hqk", grad_rows, value_all, preferred_element_type=jnp.float32
    )
    row_delta = jnp.sum(attention * grad_attention, -1, keepdims=True)
    grad_scores = (attention * (grad_attention - row_delta)).astype(jnp.bfloat16)
    grad_query = jnp.einsum(
        "hqk,khd->qhd", grad_scores, key_all, preferred_element_type=jnp.float32
    ) * score_scale + grad_rows.astype(jnp.float32)
    row_count = lax.axis_size("seq") * local_keys
    score_rows = lax.slice_in_dim(grad_scores, 0, row_count, axis=2)
    weight_rows = lax.slice_in_dim(attention_low, 0, row_count, axis=2)
    grad_key = (
        jnp.einsum("hqk,qhd->khd", score_rows, queries, preferred_element_type=jnp.float32)
        * score_scale
    )
    grad_value = jnp.einsum(
        "hqk,qhd->khd", weight_rows, grad_rows, preferred_element_type=jnp.float32
    )
    key_grads = lax.psum_scatter(
        jnp.stack(
            [grad_key.reshape(row_count, channels), grad_value.reshape(row_count, channels)], 1
        ),
        "seq",
        scatter_dimension=0,
        tiled=True,
    )
    return (
        grad_query.reshape(query_cells.shape),
        key_grads[:, 0].reshape(key_cells.shape),
        key_grads[:, 1].reshape(value_cells.shape),
    )


def shards(qkv_fine, grad_out, pool_weight, norm_gain):
    fine_cells = qkv_fine[0]
    grad_cells = grad_out[0]
    head_cells = lax.all_to_all(fine_cells, "head", split_axis=4, concat_axis=2, tiled=True)
    head_grads = lax.all_to_all(grad_cells, "head", split_axis=3, concat_axis=2, tiled=True)
    channels = head_cells.shape[-1]
    offset = lax.axis_index("head") * channels
    weight_local = lax.dynamic_slice_in_dim(pool_weight, offset, channels, 2).astype(jnp.float32)

    def head_work(normed):
        return attend(normed[0], normed[1], normed[2], head_grads)

    grad_local, grad_weight_local, grad_gain = pooled_backward(
        head_cells, weight_local, norm_gain, head_work
    )
    grad_fine = lax.all_to_all(
        grad_local.astype(jnp.bfloat16), "head", split_axis=2, concat_axis=4, tiled=True
    )
    grad_weight = lax.dynamic_update_slice_in_dim(
        jnp.zeros(pool_weight.shape, jnp.float32), grad_weight_local, offset, 2
    )
    grad_weight, grad_gain = lax.psum((grad_weight, grad_gain), ("seq", "head"))
    return (grad_fine[None], grad_weight, grad_gain)


def solution(mesh):
    in_specs = (
        P("seq", None, None, "head", None, None),
        P("seq", None, None, "head", None),
        P(),
        P(),
    )
    out_specs = (P("seq", None, None, "head", None, None), P(), P())
    return jax.shard_map(shards, mesh=mesh, in_specs=in_specs, out_specs=out_specs, check_vma=False)
```

profile of v0, /device:TPU:1, one launch (start us, length us, event | category | flops | bytes accessed | tf_op | source)
XLA Modules:
  0.0 1258.8 jit_solution(2461192312078199461)
XLA Ops:
  7.2 13.3 %copy.138 = bf16[1,4,4,8,3,768]{3,2,4,1,5,0:T(4,128)(2,1)} copy(bf16[1,4,4,8,3,768]{5,3,4,2,1,0:T(8,128)(2,1)} %param.4) | data formatting | bytes 1179648 | tf_op args[0]
  20.4 8.5 bitcast_bitcast_fusion
  29.0 12.0 reshape.3553
  41.0 7.5 all-to-all-start
  51.9 2.0 reshape.3551
  55.3 2.3 all-to-all-done
  57.5 4.4 all-to-all-start.1
  62.0 12.2 reshape.3554
  74.1 11.8 copy.223
  86.0 6.0 collective-permute-start
  92.8 2.0 collective-permute-done
  94.9 14.7 %collective-permute-start.1 = (bf16[1,5,65,3,96]{4,2,3,1,0:T(8,128)(2,1)S(1)}, bf16[1,5,65,3,96]{4,2,3,1,0:T(8,128)(2,1)S(1)}, u32[]{:S(2)}, u32[]{:S(2)}) collective-permute-start(bf16[1,5,65,3,96]{4,2,3,1,0:T(8,128)(2,1)S(1)} %pad_maximum_fusion.3), channel_id=1, source_target_pairs={{0,128},{8,136},{16,144},{24,152},{32,160},{40,168},{48,176},{56,1... | collective-permute-start | bytes 561608 | tf_op jit(solution)/shard_map/ppermute | solution.py:16
  110.3 1.3 dynamic-slice
  112.2 1.7 reshape.3552
  116.8 1.3 fusion.23
  119.4 1.2 fusion.21
  123.1 1.3 fusion.20
  125.4 82.5 %all-gather = bf16[64,1,16,96]{3,2,1,0:T(8,128)(2,1)S(1)} all-gather(bf16[1,1,16,96]{3,2,1,0:T(8,128)(2,1)S(1)} %multiply_convert_fusion.3), channel_id=2, replica_groups=mesh['seq'=64,'head'=8] {'seq'}, dimensions={0}, use_global_device_ids=true | all-gather | bytes 199680 | tf_op jit(solution)/shard_map/all_gather | solution.py:115
  212.2 62.1 %all-gather.1 = bf16[64,1,16,96]{3,2,1,0:T(8,128)(2,1)S(1)} all-gather(bf16[1,1,16,96]{3,2,1,0:T(8,128)(2,1)S(1)} %multiply_convert_fusion.2), channel_id=3, replica_groups=mesh['seq'=64,'head'=8] {'seq'}, dimensions={0}, use_global_device_ids=true | all-gather | bytes 199680 | tf_op jit(solution)/shard_map/all_gather | solution.py:116
  287.7 1.3 copy.207
  289.0 2.6 add_bitcast_fusion.2
  294.4 419.1 %all-reduce.262.cloned.1.call-done = f32[1024,2,96]{2,1,0:T(2,128)} async-done(((f32[1024,2,96]{2,1,0:T(2,128)}), f32[1024,2,96]{2,1,0:T(2,128)}) %all-reduce.262.cloned.1.call-update) | async-done | bytes 786448
  724.8 1.2 add_bitcast_fusion.1
  727.4 1.3 collective-permute-start.2
  731.2 16.8 %collective-permute-done.2 = bf16[1,5,65,3,96]{4,1,2,0,3:T(8,128)(2,1)S(1)} collective-permute-done((bf16[1,5,65,3,96]{4,1,2,0,3:T(8,128)(2,1)S(1)}, bf16[1,5,65,3,96]{4,1,2,0,3:T(8,128)(2,1)S(1)}, u32[]{:S(2)}, u32[]{:S(2)}) %collective-permute-start.2) | collective-permute-done | bytes 187232 | tf_op jit(solution)/shard_map/ppermute | solution.py:16
  748.5 4.1 collective-permute-start.3
  753.4 23.0 %collective-permute-done.3 = bf16[4,1,65,3,96]{4,1,2,0,3:T(2,128)(2,1)S(1)} collective-permute-done((bf16[4,1,65,3,96]{4,1,2,0,3:T(2,128)(2,1)S(1)}, bf16[4,1,65,3,96]{4,1,2,0,3:T(2,128)(2,1)S(1)}, u32[]{:S(2)}, u32[]{:S(2)}) %collective-permute-start.3) | collective-permute-done | bytes 149792 | tf_op jit(solution)/shard_map/ppermute | solution.py:16
  779.4 6.1 all-to-all-start.2
  787.0 109.2 %psum.15 = f32[3,96]{1,0:T(4,128)} all-reduce(f32[3,96]{1,0:T(4,128)S(1)} %pad_add_fusion.2), channel_id=1, replica_groups=mesh['seq'=64,'head'=8] {'seq','head'}, use_global_device_ids=true, to_apply=%region_100.101 | all-reduce | flops 288 | bytes 2304 | tf_op jit(solution)/shard_map/psum | solution.py:181
  896.6 1.5 broadcast_in_dim.648
  898.1 352.2 %all-reduce.260.cloned.1.call-done = f32[27,3,768]{2,0,1:T(8,128)} async-done(((f32[27,3,768]{2,0,1:T(8,128)}), f32[27,3,768]{2,0,1:T(8,128)}) %all-reduce.260.cloned.1.call-update) | async-done | bytes 248848 | tf_op jit(solution)/shard_map/psum | solution.py:181
  1250.3 1.7 copy.305
  (516 shorter events, 52.6 us)
Async XLA Ops:
  41.0 16.5 %all-to-all-start = ((bf16[8,2,18432]{2,1,0:T(2,128)(2,1)}), bf16[8,2,18432]{2,1,0:T(2,128)(2,1)S(1)}, u32[]{:S(2)}, u32[]{:S(2)}) async-start(bf16[8,2,18432]{2,1,0:T(2,128)(2,1)} %reshape.3553), calls=%async_computation | async-start | bytes 1179648 | tf_op jit(solution)/shard_map/all_to_all | solution.py:163
  57.5 54.7 %all-to-all-start.1 = ((bf16[8,2,768]{2,1,0:T(2,128)(2,1)}), bf16[8,2,768]{2,1,0:T(2,128)(2,1)S(1)}, u32[]{:S(2)}, u32[]{:S(2)}) async-start(bf16[8,2,768]{2,1,0:T(2,128)(2,1)} %reshape.3551), calls=%async_computation.1 | async-start | bytes 49152 | tf_op jit(solution)/shard_map/all_to_all | solution.py:164
  61.9 651.6 %all-reduce.262.cloned.1.call-start = ((), (), s32[]{:S(2)}) async-start(), calls=%async_computation.4 | async-start | bytes 2097152
  86.0 8.8 collective-permute-start
  94.9 20.2 %collective-permute-start.1 = (bf16[1,5,65,3,96]{4,2,3,1,0:T(8,128)(2,1)S(1)}, bf16[1,5,65,3,96]{4,2,3,1,0:T(8,128)(2,1)S(1)}, u32[]{:S(2)}, u32[]{:S(2)}) collective-permute-start(bf16[1,5,65,3,96]{4,2,3,1,0:T(8,128)(2,1)S(1)} %pad_maximum_fusion.3), channel_id=1, source_target_pairs={{0,128},{8,136},{16,144},{24,152},{32,160},{40,168},{48,176},{56,1... | collective-permute-start | bytes 561608 | tf_op jit(solution)/shard_map/ppermute | solution.py:16
  293.2 427.1 %copy-start.43 = (f32[96]{0:T(128)S(1)}, f32[96]{0:T(128)}, u32[]{:S(2)}) copy-start(f32[96]{0:T(128)} %get-tuple-element.223) | copy-start | bytes 1156
  293.2 427.1 %copy-start.45 = (f32[96]{0:T(128)S(1)}, f32[96]{0:T(128)}, u32[]{:S(2)}) copy-start(f32[96]{0:T(128)} %get-tuple-element.224) | copy-start | bytes 1156
  293.3 427.1 %copy-start.47 = (f32[96]{0:T(128)S(1)}, f32[96]{0:T(128)}, u32[]{:S(2)}) copy-start(f32[96]{0:T(128)} %get-tuple-element.225) | copy-start | bytes 1156
  293.3 427.1 %copy-start.49 = (f32[96]{0:T(128)S(1)}, f32[96]{0:T(128)}, u32[]{:S(2)}) copy-start(f32[96]{0:T(128)} %get-tuple-element.226) | copy-start | bytes 1156
  293.3 427.1 %copy-start.51 = (f32[96]{0:T(128)S(1)}, f32[96]{0:T(128)}, u32[]{:S(2)}) copy-start(f32[96]{0:T(128)} %get-tuple-element.227) | copy-start | bytes 1156
  293.3 427.1 %copy-start.53 = (f32[96]{0:T(128)S(1)}, f32[96]{0:T(128)}, u32[]{:S(2)}) copy-start(f32[96]{0:T(128)} %get-tuple-element.228) | copy-start | bytes 1156
  293.3 427.1 %copy-start.55 = (f32[96]{0:T(128)S(1)}, f32[96]{0:T(128)}, u32[]{:S(2)}) copy-start(f32[96]{0:T(128)} %get-tuple-element.229) | copy-start | bytes 1156
  293.3 427.1 %copy-start.57 = (f32[96]{0:T(128)S(1)}, f32[96]{0:T(128)}, u32[]{:S(2)}) copy-start(f32[96]{0:T(128)} %get-tuple-element.230) | copy-start | bytes 1156
  293.3 427.1 %copy-start.59 = (f32[96]{0:T(128)S(1)}, f32[96]{0:T(128)}, u32[]{:S(2)}) copy-start(f32[96]{0:T(128)} %get-tuple-element.231) | copy-start | bytes 1156
  293.3 427.1 %copy-start.95 = (f32[96]{0:T(128)S(1)}, f32[96]{0:T(128)}, u32[]{:S(2)}) copy-start(f32[96]{0:T(128)} %get-tuple-element.204) | copy-start | bytes 1156
  293.3 427.1 %copy-start.97 = (f32[96]{0:T(128)S(1)}, f32[96]{0:T(128)}, u32[]{:S(2)}) copy-start(f32[96]{0:T(128)} %get-tuple-element.214) | copy-start | bytes 1156
  293.3 427.1 %copy-start.99 = (f32[96]{0:T(128)S(1)}, f32[96]{0:T(128)}, u32[]{:S(2)}) copy-start(f32[96]{0:T(128)} %get-tuple-element.215) | copy-start | bytes 1156
  293.4 427.1 %copy-start.101 = (f32[96]{0:T(128)S(1)}, f32[96]{0:T(128)}, u32[]{:S(2)}) copy-start(f32[96]{0:T(128)} %get-tuple-element.216) | copy-start | bytes 1156
  293.4 427.1 %copy-start.103 = (f32[96]{0:T(128)S(1)}, f32[96]{0:T(128)}, u32[]{:S(2)}) copy-start(f32[96]{0:T(128)} %get-tuple-element.217) | copy-start | bytes 1156
  293.4 428.0 %copy-start.77 = (f32[96]{0:T(128)S(1)}, f32[96]{0:T(128)}, u32[]{:S(2)}) copy-start(f32[96]{0:T(128)} %get-tuple-element.205) | copy-start | bytes 1156
  293.4 428.0 %copy-start.79 = (f32[96]{0:T(128)S(1)}, f32[96]{0:T(128)}, u32[]{:S(2)}) copy-start(f32[96]{0:T(128)} %get-tuple-element.206) | copy-start | bytes 1156
  293.4 428.0 %copy-start.81 = (f32[96]{0:T(128)S(1)}, f32[96]{0:T(128)}, u32[]{:S(2)}) copy-start(f32[96]{0:T(128)} %get-tuple-element.207) | copy-start | bytes 1156
  293.4 428.0 %copy-start.83 = (f32[96]{0:T(128)S(1)}, f32[96]{0:T(128)}, u32[]{:S(2)}) copy-start(f32[96]{0:T(128)} %get-tuple-element.208) | copy-start | bytes 1156
  293.4 428.0 %copy-start.85 = (f32[96]{0:T(128)S(1)}, f32[96]{0:T(128)}, u32[]{:S(2)}) copy-start(f32[96]{0:T(128)} %get-tuple-element.209) | copy-start | bytes 1156
  293.4 428.0 %copy-start.87 = (f32[96]{0:T(128)S(1)}, f32[96]{0:T(128)}, u32[]{:S(2)}) copy-start(f32[96]{0:T(128)} %get-tuple-element.210) | copy-start | bytes 1156
  293.5 428.0 %copy-start.89 = (f32[96]{0:T(128)S(1)}, f32[96]{0:T(128)}, u32[]{:S(2)}) copy-start(f32[96]{0:T(128)} %get-tuple-element.211) | copy-start | bytes 1156
  293.5 428.0 %copy-start.91 = (f32[96]{0:T(128)S(1)}, f32[96]{0:T(128)}, u32[]{:S(2)}) copy-start(f32[96]{0:T(128)} %get-tuple-element.212) | copy-start | bytes 1156
  293.5 428.0 %copy-start.93 = (f32[96]{0:T(128)S(1)}, f32[96]{0:T(128)}, u32[]{:S(2)}) copy-start(f32[96]{0:T(128)} %get-tuple-element.213) | copy-start | bytes 1156
  727.4 20.6 %collective-permute-start.2 = (bf16[1,5,65,3,96]{4,1,2,0,3:T(8,128)(2,1)S(1)}, bf16[1,5,65,3,96]{4,1,2,0,3:T(8,128)(2,1)S(1)}, u32[]{:S(2)}, u32[]{:S(2)}) collective-permute-start(bf16[1,5,65,3,96]{4,1,2,0,3:T(8,128)(2,1)S(1)} %slice.1666), channel_id=1, source_target_pairs={{128,0},{136,8},{144,16},{152,24},{160,32},{168,40},{176,48},{184,... | collective-permute-start | bytes 561608 | tf_op jit(solution)/shard_map/ppermute | solution.py:16
  748.5 27.9 %collective-permute-start.3 = (bf16[4,1,65,3,96]{4,1,2,0,3:T(2,128)(2,1)S(1)}, bf16[4,1,65,3,96]{4,1,2,0,3:T(2,128)(2,1)S(1)}, u32[]{:S(2)}, u32[]{:S(2)}) collective-permute-start(bf16[4,1,65,3,96]{4,1,2,0,3:T(2,128)(2,1)S(1)} %fusion.9), channel_id=1, source_target_pairs={{8,0},{16,8},{24,16},{32,24},{40,32},{48,40},{56,48},{64,56},{72,6... | collective-permute-start | bytes 449288 | tf_op jit(solution)/shard_map/ppermute | solution.py:16
  779.4 116.8 %all-to-all-start.2 = ((bf16[4,4,64,3,96]{4,1,0,3,2:T(4,128)(2,1)}), bf16[4,4,64,3,96]{4,1,0,3,2:T(4,128)(2,1)S(1)}, u32[]{:S(2)}, u32[]{:S(2)}) async-start(bf16[4,4,64,3,96]{4,1,0,3,2:T(4,128)(2,1)} %copy.218), calls=%async_computation.2 | async-start | bytes 1572864 | tf_op jit(solution)/shard_map/all_to_all | solution.py:175
  785.5 464.8 %all-reduce.260.cloned.1.call-start = ((), (), s32[]{:S(2)}) async-start(), calls=%async_computation.3 | async-start | bytes 589824 | tf_op jit(solution)/shard_map/psum | solution.py:181
  (137 other events, 10477.7 us)
Sparse Core Ops, SparseCore 0:
  289.1 424.3 all-reduce.261
  793.3 456.9 all-reduce.259
where the time goes:
time: 1260 us
  waiting for transfers between devices  815 us (65%)
  blocking collectives  254 us (20%)
  local copies, waits for them, and re-layouts  99.1 us (8%)
  starting transfers between devices  44.1 us (4%)
  other arithmetic  26.8 us (2%)
  between operations  18.1 us (1%)
    unnamed x3, waiting for transfers between devices  419 us
    psum x1, waiting for transfers between devices, shards(): grad_weight, grad_gain = lax.psum((grad_weight, grad_gain), ('seq', 'head'))  352 us
    psum x1, blocking collectives, shards(): grad_weight, grad_gain = lax.psum((grad_weight, grad_gain), ('seq', 'head'))  109 us
    all_gather x1, blocking collectives, attend(): lax.all_gather(key_part, 'seq', axis=0, tiled=True)  82.5 us
    all_gather x1, blocking collectives, attend(): lax.all_gather(value_part, 'seq', axis=0, tiled=True)  62.1 us
    unnamed x334, local copies, waits for them, and re-layouts  57 us
    ppermute x4, waiting for transfers between devices, from_behind(): return lax.ppermute(block, axis, route)  41.8 us
    ppermute x4, starting transfers between devices, from_behind(): return lax.ppermute(block, axis, route)  26 us
  transfers between devices with their start and end apart: 9, of which 6 were waited for; matrix products, arithmetic and copies ran while one was open for 4% of the time, Pallas kernels for 0%

commit v1 on v0

v1 whole, which is shorter than its diff:
```python
import jax
import jax.numpy as jnp
from jax import lax
from jax.experimental import pallas as pl
from jax.experimental.pallas import tpu as pltpu
from jax.sharding import PartitionSpec as P

MESH = pl.DeviceIdType.MESH
F32 = jnp.float32
BF16 = jnp.bfloat16
HD = 96
HEADS = 8
ROW_GROUPS = 16
SEQ = 64
ZS = 16
SCALE = HD ** -0.5

PAIRS_Q = (((0, 1), (1, 2)), ((1, 0), (2, 1), (3, 2)), ((3, 0),))
PAIRS_K = (((0, 1), (1, 2)), ((3, 0),))
OWN_Q = (0, 1, 3, 4)

(A2A_P, A2A_G, FWD_ROW, FWD_FRAME, FWD_CORNER, GATHER, QUAD, STATS, DQ, SCATTER,
 BWD_ROW, BWD_FRAME, BWD_CORNER, A2A_B, SUM_PLANE, SUM_Z, SPREAD) = range(17)


def iota(shape, dim):
    return lax.broadcasted_iota(jnp.int32, shape, dim)


def up(x, by):
    size = x.shape[0]
    return pltpu.roll(x, (size - by) % size, 0)


def split_heads(tiles):
    lane = iota(tiles[0].shape, 1)
    heads = []
    for n in range(HEADS):
        t = tiles[n // 4 * 3:n // 4 * 3 + 3]
        if n % 4 == 0:
            v = t[0]
        elif n % 4 == 1:
            v = jnp.where(lane < 32, pltpu.roll(t[0], 32, 1), pltpu.roll(t[1], 32, 1))
        elif n % 4 == 2:
            v = jnp.where(lane < 64, pltpu.roll(t[1], 64, 1), pltpu.roll(t[2], 64, 1))
        else:
            v = pltpu.roll(t[2], 96, 1)
        heads.append(jnp.where(lane < HD, v, 0.0))
    return heads


def merge_heads(h):
    lane = iota(h[0].shape, 1)
    tiles = []
    for half in (0, 4):
        a, b, c, d = h[half:half + 4]
        tiles.append(jnp.where(lane < 96, a, pltpu.roll(b, 96, 1)))
        tiles.append(jnp.where(lane < 64, pltpu.roll(b, 96, 1), pltpu.roll(c, 64, 1)))
        tiles.append(jnp.where(lane < 32, pltpu.roll(c, 64, 1), pltpu.roll(d, 32, 1)))
    return tiles


def tiles_of(v):
    return [v[:, j * 128:(j + 1) * 128] for j in range(6)]


def kernel(x_ref, g_ref, w_ref, gain_ref, gx_ref, gw_ref, gg_ref,
           wt, sb, gs, rb, gr, pe, hs, hr, norm, kvg, qgr, raised_ref, ga_ref, st, dqb, dqr, zb, zr,
           hb, hbr, ge, sb2, rb2, gall, ex, sw, wb, kr, zs, fr, flat, gsc, ss, rs):
    s = lax.axis_index("seq")
    n = lax.axis_index("head")
    group, u = s // ROW_GROUPS, s % ROW_GROUPS
    yl, z, core = s // (2 * ZS), s // 2 % ZS, s % 2

    def head_peer(k):
        return (s, lax.rem(n + k, HEADS))

    def z_peer(k):
        return (yl * (2 * ZS) + lax.rem(z + k, ZS) * 2 + core, n)

    def quad_seq(k):
        return lax.rem(yl + k // 2, 2) * (2 * ZS) + z * 2 + lax.rem(core + k % 2, 2)

    def plane_peer(p):
        return (quad_seq(p // HEADS), lax.rem(n + p % HEADS, HEADS))

    def seq_peer(d):
        return (lax.rem(s + d + SEQ, SEQ), n)

    barrier = pltpu.get_barrier_semaphore()

    def greet(peer):
        pl.semaphore_signal(barrier, inc=1, device_id=peer, device_id_type=MESH)

    def each(count, body):
        def step(k, carry):
            body(k)
            return carry
        lax.fori_loop(1, count, step, 0)

    each(32, lambda p: greet(plane_peer(p)))
    each(ZS, lambda k: greet(z_peer(k)))
    for d in (1, 16, 17, -1, -16, -17):
        greet(seq_peer(d))

    def send(stage, src, dst, peer):
        pltpu.make_async_remote_copy(src_ref=src, dst_ref=dst, send_sem=ss.at[stage], recv_sem=rs.at[stage],
                                     device_id=peer, device_id_type=MESH).start()

    def arrived(stage, ref):
        pltpu.make_async_copy(ref, ref, rs.at[stage]).wait()

    def sent(stage, ref):
        pltpu.make_async_copy(ref, ref, ss.at[stage]).wait()

    row = iota((8, 768), 0)

    def taps(ab, carry):
        def one(m, e):
            return jnp.broadcast_to(w_ref[m, pl.ds(ab * 3 + e, 1), :], (8, 768))
        wt[0, ab] = jnp.where(row % 2 == 0, one(0, 1), one(0, 2))
        wt[1, ab] = jnp.where(row % 2 == 1, one(0, 0), 0.0)
        for m in (1, 2):
            wt[1 + m, ab] = jnp.where(row % 4 == 0, one(m, 1), jnp.where(
                row % 4 == 1, one(m, 2), jnp.where(row % 4 == 3, one(m, 0), 0.0)))
        return carry
    lax.fori_loop(0, 9, taps, 0)

    def fine(m, f, r):
        return x_ref[f, r, m].astype(F32)

    def store_heads(grp, v):
        for h, part in enumerate(split_heads(tiles_of(v))):
            sb[h, grp * 8:grp * 8 + 8, :] = part

    for t in range(3):
        for y in range(3):
            a_sum = b_sum = None
            for f, a in PAIRS_Q[t]:
                for r, b in PAIRS_Q[y]:
                    v = fine(0, f, r)
                    ta, tb = v * wt[0, a * 3 + b], v * wt[1, a * 3 + b]
                    a_sum = ta if a_sum is None else a_sum + ta
                    b_sum = tb if b_sum is None else b_sum + tb
            b1 = pltpu.roll(b_sum, 1, 0)
            e = a_sum + up(a_sum, 1) + jnp.where(row == 0, 0.0, b1)
            v = jnp.where(row == 0, e, jnp.where(row == 1, up(e, 1), jnp.where(row == 2, up(e, 2), jnp.where(
                row == 3, up(e, 3), jnp.where(row == 4, up(b1, 4), 0.0)))))
            store_heads(t * 3 + y, v)
    for t in range(2):
        for y in range(2):
            both = []
            for m in (1, 2):
                k_sum = None
                for f, a in PAIRS_K[t]:
                    for r, b in PAIRS_K[y]:
                        tk = fine(m, f, r) * wt[1 + m, a * 3 + b]
                        k_sum = tk if k_sum is None else k_sum + tk
                t1 = k_sum + up(k_sum, 1)
                both.append(jnp.where(row == 0, t1, jnp.where(row == 1, up(t1, 2) + up(k_sum, 4), jnp.where(
                    row == 2, up(k_sum, 5), 0.0))))
            store_heads(9 + t * 2 + y, both[0] + pltpu.roll(both[1], 4, 0))
    gh = []
    for t in range(2):
        v = jnp.concatenate([g_ref[t, 0].astype(F32), g_ref[t, 1].astype(F32)], 0)
        gh.append(split_heads(tiles_of(v)))
    for h in range(HEADS):
        gs[h] = jnp.concatenate([gh[0][h], gh[1][h]], 0).astype(BF16)

    pl.semaphore_wait(barrier, 31 + ZS - 1 + 6)

    def to_heads(k):
        peer = head_peer(k)
        send(A2A_P, sb.at[peer[1]], rb.at[k], peer)
        send(A2A_G, gs.at[peer[1]], gr.at[k], peer)
    each(HEADS, to_heads)
    rb[0] = sb[n]
    gr[0] = gs[n]
    arrived(A2A_P, rb.at[pl.ds(1, HEADS - 1)])
    arrived(A2A_G, gr.at[pl.ds(1, HEADS - 1)])

    row8 = iota((8, 128), 0)
    from_col = [lax.rem(n - h + HEADS, HEADS) for h in range(HEADS)]
    for grp in range(9):
        parts = [rb[from_col[h], grp * 8:grp * 8 + 8, :] for h in range(HEADS)]
        rolled = [pltpu.roll(parts[2 * j + 1], 4, 0) for j in range(4)]
        for j in range(4):
            v = parts[2 * j] + jnp.where(row8 >= 4, rolled[j], 0.0)
            if j:
                v = v + jnp.where(row8 == 0, rolled[j - 1], 0.0)
            pe[grp * 32 + j * 8:grp * 32 + j * 8 + 8, :] = v
    for grp in range(4):
        parts = [rb[from_col[h], 72 + grp * 8:80 + grp * 8, :] for h in range(HEADS)]
        for m in range(2):
            if m == 0:
                own = [jnp.where(row8 < 4, p, 0.0) for p in parts]
            else:
                own = [pltpu.roll(jnp.where(row8 >= 4, p, 0.0), 4, 0) for p in parts]
            last = [pltpu.roll(own[4 * j + 3], 6, 0) for j in range(2)]
            for j in range(2):
                v = own[4 * j] + pltpu.roll(own[4 * j + 1], 2, 0) + pltpu.roll(own[4 * j + 2], 4, 0)
                v = v + jnp.where(row8 >= 4, last[j], 0.0)
                if j:
                    v = v + jnp.where(row8 == 0, last[0], 0.0)
                at = 288 + m * 64 + grp * 16 + j * 8
                pe[at:at + 8, :] = v

    def pq(t, y):
        return pe[(t * 3 + y) * 32:(t * 3 + y) * 32 + 32, :]

    def pkv(m, t, y):
        at = 288 + m * 64 + (t * 2 + y) * 16
        return pe[at:at + 16, :]

    hs[0:96, :] = jnp.concatenate([pq(0, 2), pq(1, 2), pkv(0, 0, 1), pkv(1, 0, 1)], 0).astype(BF16)
    hs[96:192, :] = jnp.concatenate([pq(2, 0), pq(2, 1), pkv(0, 1, 0), pkv(1, 1, 0)], 0).astype(BF16)
    hs[192:256, :] = jnp.concatenate([pq(2, 2), pkv(0, 1, 1), pkv(1, 1, 1)], 0).astype(BF16)
    spans = (pl.ds(0, 96), pl.ds(96, 96), pl.ds(192, 64))
    for stage, span, d in zip((FWD_ROW, FWD_FRAME, FWD_CORNER), spans, (1, 16, 17)):
        send(stage, hs.at[span], hr.at[span], seq_peer(d))

    parts = [gr[from_col[h]].astype(F32) for h in range(HEADS)]
    for t in range(2):
        for y in range(2):
            vs = []
            for j in range(4):
                a, b = parts[2 * j][t * 8:t * 8 + 8], parts[2 * j + 1][t * 8:t * 8 + 8]
                if y == 0:
                    vs.append(jnp.where(row8 < 4, a, pltpu.roll(b, 4, 0)))
                else:
                    vs.append(jnp.where(row8 < 4, pltpu.roll(a, 4, 0), b))
            at = 128 + (t * 2 + y) * 32
            qgr[0, at:at + 32, :] = jnp.concatenate(vs, 0).astype(BF16)
    gsc[...] = jnp.zeros_like(gsc)
    gsc[0:3, 0:HD] = gain_ref[...]

    for stage, span in zip((FWD_ROW, FWD_FRAME, FWD_CORNER), spans):
        arrived(stage, hr.at[span])
    has_u = (u > 0).astype(F32)
    has_g = (group > 0).astype(F32)

    def border(lo, count, has):
        return hr[lo:lo + count, :].astype(F32) * has

    has_c = has_u * has_g
    q00 = pq(0, 0) + border(0, 32, has_u) + border(96, 32, has_g) + border(192, 32, has_c)
    q01 = pq(0, 1) + border(128, 32, has_g)
    q10 = pq(1, 0) + border(32, 32, has_u)
    k00 = pkv(0, 0, 0) + border(64, 16, has_u) + border(160, 16, has_g) + border(224, 16, has_c)
    v00 = pkv(1, 0, 0) + border(80, 16, has_u) + border(176, 16, has_g) + border(240, 16, has_c)
    pooled = jnp.concatenate([q00, q01, q10, pq(1, 1), k00, v00], 0)
    lane = iota((160, 128), 1)
    which = iota((160, 128), 0)
    gain = jnp.where(which < 128, gsc[0:1, :], jnp.where(which < 144, gsc[1:2, :], gsc[2:3, :]))
    centred = jnp.where(lane < HD, pooled - jnp.sum(pooled, 1, keepdims=True) * (1.0 / HD), 0.0)
    rstd = lax.rsqrt(jnp.sum(centred * centred, 1, keepdims=True) * (1.0 / HD) + 1e-6)
    unit = centred * rstd
    normed = (unit * gain).astype(BF16)
    norm[0] = unit
    norm[1] = jnp.broadcast_to(rstd, (160, 128))
    norm[2] = gain
    qgr[0, 0:128, :] = normed[0:128]
    kvg[0] = normed[128:160]

    each(ZS, lambda k: send(GATHER, kvg.at[0], kvg.at[k], z_peer(k)))
    for k in range(1, 4):
        send(QUAD, qgr.at[0], qgr.at[k], (quad_seq(k), n))
    arrived(QUAD, qgr.at[pl.ds(1, 3)])
    arrived(GATHER, kvg.at[pl.ds(1, ZS - 1)])

    keys = kvg[:, 0:16, :].reshape(256, 128)
    values = kvg[:, 16:32, :].reshape(256, 128)
    queries = qgr[:, 0:128, :].reshape(512, 128)
    grads = qgr[:, 128:256, :].reshape(512, 128)
    nt = (((1,), (1,)), ((), ()))
    raised_ref[...] = jnp.exp(lax.dot_general(keys, queries, nt, preferred_element_type=F32) * SCALE)
    ga_ref[...] = lax.dot_general(values, grads, nt, preferred_element_type=F32)
    total = jnp.sum(raised_ref[...], 0, keepdims=True)
    delta = jnp.sum(raised_ref[...] * ga_ref[...], 0, keepdims=True)
    for j in range(4):
        st[0, j:j + 1, :] = total[:, j * 128:(j + 1) * 128]
        st[0, 4 + j:5 + j, :] = delta[:, j * 128:(j + 1) * 128]
    for k in range(1, 4):
        send(STATS, st.at[0], st.at[k], (quad_seq(k), n))
    arrived(STATS, st.at[pl.ds(1, 3)])

    def quad_sum(at):
        outs = []
        for j in range(4):
            v = st[0, at + j:at + j + 1, :]
            for k in range(1, 4):
                i = at + (j ^ k)
                v = v + st[k, i:i + 1, :]
            outs.append(v)
        return jnp.concatenate(outs, 1)

    inverse = 1.0 / quad_sum(0)
    row_delta = quad_sum(4) * inverse
    attention = raised_ref[...] * inverse
    grad_scores = (attention * (ga_ref[...] - row_delta)).astype(BF16)
    grad_query = lax.dot_general(grad_scores, keys, (((0,), (0,)), ((), ())), preferred_element_type=F32)
    dqb[...] = grad_query.reshape(4, 128, 128)
    for k in range(1, 4):
        send(DQ, dqb.at[k], dqr.at[k], (quad_seq(k), n))
    grad_key = jnp.dot(grad_scores, queries, preferred_element_type=F32) * SCALE
    grad_value = jnp.dot(attention.astype(BF16), grads, preferred_element_type=F32)
    zb[:, 0:16, :] = grad_key.reshape(ZS, 16, 128).astype(zb.dtype)
    zb[:, 16:32, :] = grad_value.reshape(ZS, 16, 128).astype(zb.dtype)
    each(ZS, lambda k: send(SCATTER, zb.at[k], zr.at[k], z_peer(ZS - k)))
    zr[0] = zb[0]
    dqr[0] = dqb[0]
    arrived(DQ, dqr.at[pl.ds(1, 3)])
    arrived(SCATTER, zr.at[pl.ds(1, ZS - 1)])

    dq = dqr[0] + dqr[1] + dqr[2] + dqr[3]
    dkv = jnp.sum(zr[...].astype(F32), 0)
    grad_normed = jnp.concatenate([dq * SCALE + qgr[0, 128:256, :].astype(F32), dkv], 0)
    unit = norm[0]
    gain_rows = grad_normed * unit
    gsc[0:1, :] = jnp.sum(gain_rows[0:128], 0, keepdims=True)
    gsc[1:2, :] = jnp.sum(gain_rows[128:144], 0, keepdims=True)
    gsc[2:3, :] = jnp.sum(gain_rows[144:160], 0, keepdims=True)
    inner = grad_normed * norm[2]
    mean_1 = jnp.sum(inner, 1, keepdims=True) * (1.0 / HD)
    mean_2 = jnp.sum(inner * unit, 1, keepdims=True) * (1.0 / HD)
    grad_pooled = norm[1] * jnp.where(lane < HD, inner - mean_1 - unit * mean_2, 0.0)

    qg = [grad_pooled[i * 32:i * 32 + 32] for i in range(4)]
    kvgr = grad_pooled[128:160]
    hb[0:96, :] = jnp.concatenate([qg[0], qg[2], kvgr], 0).astype(BF16)
    hb[96:192, :] = jnp.concatenate([qg[0], qg[1], kvgr], 0).astype(BF16)
    hb[192:256, :] = jnp.concatenate([qg[0], kvgr], 0).astype(BF16)
    for stage, span, d in zip((BWD_ROW, BWD_FRAME, BWD_CORNER), spans, (-1, -16, -17)):
        send(stage, hb.at[span], hbr.at[span], seq_peer(d))
    for i, grp in enumerate(OWN_Q):
        ge[grp * 32:grp * 32 + 32, :] = qg[i]
    ge[288:304, :] = kvgr[0:16]
    ge[352:368, :] = kvgr[16:32]
    for stage, span in zip((BWD_ROW, BWD_FRAME, BWD_CORNER), spans):
        arrived(stage, hbr.at[span])
    has_u = (u < ROW_GROUPS - 1).astype(F32)
    has_g = (group < SEQ // ROW_GROUPS - 1).astype(F32)

    def returned(lo, count, has):
        return hbr[lo:lo + count, :].astype(F32) * has

    has_c = has_u * has_g
    ge[2 * 32:3 * 32, :] = returned(0, 32, has_u)
    ge[5 * 32:6 * 32, :] = returned(32, 32, has_u)
    ge[6 * 32:7 * 32, :] = returned(96, 32, has_g)
    ge[7 * 32:8 * 32, :] = returned(128, 32, has_g)
    ge[8 * 32:9 * 32, :] = returned(192, 32, has_c)
    for m in range(2):
        at = 288 + m * 64
        ge[at + 16:at + 32, :] = returned(64 + 16 * m, 16, has_u)
        ge[at + 32:at + 48, :] = returned(160 + 16 * m, 16, has_g)
        ge[at + 48:at + 64, :] = returned(224 + 16 * m, 16, has_c)

    zero = jnp.zeros((8, 128), F32)
    out_rows = [[] for _ in range(HEADS)]
    for grp in range(9):
        vs = [ge[grp * 32 + j * 8:grp * 32 + j * 8 + 8, :] for j in range(4)] + [zero]
        half = [pltpu.roll(v, 4, 0) for v in vs]
        for h in range(HEADS):
            j = h // 2
            out_rows[h].append(vs[j] if h % 2 == 0 else jnp.where(row8 < 4, half[j], half[j + 1]))
    for grp in range(4):
        vs = [[ge[at:at + 8, :] for at in (288 + m * 64 + grp * 16, 296 + m * 64 + grp * 16)] + [zero] for m in range(2)]
        for h in range(HEADS):
            j, i = h // 4, h % 4
            parts = []
            for m in range(2):
                v = pltpu.roll(vs[m][j], 8 - 2 * i, 0) if i else vs[m][j]
                if i == 3:
                    v = jnp.where(row8 < 2, v, pltpu.roll(vs[m][j + 1], 2, 0))
                parts.append(v)
            out_rows[h].append(jnp.where(row8 < 4, parts[0], pltpu.roll(parts[1], 4, 0)))
    for h in range(HEADS):
        sb2[h] = jnp.concatenate(out_rows[h] + [zero], 0).astype(BF16)

    def to_columns(k):
        peer = head_peer(k)
        send(A2A_B, sb2.at[peer[1]], rb2.at[k], peer)
    each(HEADS, to_columns)
    rb2[0] = sb2[n]
    arrived(A2A_B, rb2.at[pl.ds(1, HEADS - 1)])

    tiles = merge_heads([rb2[from_col[h]].astype(F32) for h in range(HEADS)])
    for j in range(6):
        gall[:, j * 128:(j + 1) * 128] = tiles[j].astype(BF16)
    r = iota((208, 112), 0)
    grp, second, i = r >> 4, (r >> 3) & 1, r & 7
    target = grp * 8 + jnp.where(grp < 9, (i >> 1) + second, ((i + 1) >> 2) + 4 * second)
    spread = jnp.where(iota((208, 112), 1) == target, 1.0, 0.0).astype(BF16)
    ex[...] = jnp.dot(spread, gall[...], preferred_element_type=F32)

    def g_at(grp, second):
        at = grp * 16 + second * 8
        return ex[at:at + 8, :]

    def pairs(pair_list, a):
        return [(f, t) for t, entries in enumerate(pair_list) for f, tap in entries if tap == a]

    for a in range(3):
        for b in range(3):
            sums = [None] * 4
            for f, t in pairs(PAIRS_Q, a):
                for rr, y in pairs(PAIRS_Q, b):
                    v = fine(0, f, rr)
                    for second in range(2):
                        term = v * g_at(t * 3 + y, second)
                        sums[second] = term if sums[second] is None else sums[second] + term
            for f, t in pairs(PAIRS_K, a):
                for rr, y in pairs(PAIRS_K, b):
                    for m in (1, 2):
                        term = fine(m, f, rr) * g_at(9 + t * 2 + y, m - 1)
                        sums[1 + m] = term if sums[1 + m] is None else sums[1 + m] + term
            for i in range(4):
                sw[i, a * 3 + b] = sums[i]

    wb[480:512, :] = jnp.zeros((32, 128), F32)
    wb[486:489, :] = gsc[0:3, :]

    def by_tap(ab, carry):
        for m in range(3):
            if m == 0:
                first, second = sw[0, ab], sw[1, ab]
                e_rows = (jnp.where(row % 2 == 1, second, 0.0), jnp.where(row % 2 == 0, first, 0.0),
                          jnp.where(row % 2 == 1, first, 0.0))
            else:
                v = sw[1 + m, ab]
                e_rows = tuple(jnp.where(row % 4 == c, v, 0.0) for c in (3, 0, 1))
            for e in range(3):
                v = jnp.sum(e_rows[e], 0, keepdims=True)
                for j in range(6):
                    wb[pl.ds(j * 81 + m * 27 + ab * 3 + e, 1), :] = v[:, j * 128:(j + 1) * 128]
        return carry
    lax.fori_loop(0, 9, by_tap, 0)

    def piece_of(p):
        quad = lax.rem(yl + p // 16, 2) * 2 + lax.rem(core + p // 8 % 2, 2)
        return quad * HEADS + lax.rem(n + p % HEADS, HEADS)

    def piece(p):
        return pl.ds(pl.multiple_of(piece_of(p) * 16, 16), 16)

    each(32, lambda p: send(SUM_PLANE, wb.at[piece(p)], kr.at[p], plane_peer(p)))
    kr[0] = wb[piece(0), :]

    for f in range(4):
        for rr in range(4):
            q_sum = None
            for t, a in [(t, a) for t, entries in enumerate(PAIRS_Q) for ff, a in entries if ff == f]:
                for y, b in [(y, b) for y, entries in enumerate(PAIRS_Q) for ff, b in entries if ff == rr]:
                    term = g_at(t * 3 + y, 0) * wt[0, a * 3 + b] + g_at(t * 3 + y, 1) * wt[1, a * 3 + b]
                    q_sum = term if q_sum is None else q_sum + term
            gx_ref[f, rr, 0] = q_sum.astype(BF16)
            for m in (1, 2):
                k_sum = jnp.zeros((8, 768), F32)
                for t, a in [(t, a) for t, entries in enumerate(PAIRS_K) for ff, a in entries if ff == f]:
                    for y, b in [(y, b) for y, entries in enumerate(PAIRS_K) for ff, b in entries if ff == rr]:
                        k_sum = g_at(9 + t * 2 + y, m - 1) * wt[1 + m, a * 3 + b]
                gx_ref[f, rr, m] = k_sum.astype(BF16)

    arrived(SUM_PLANE, kr.at[pl.ds(1, 31)])
    zs[0] = jnp.sum(kr[...], 0)
    each(ZS, lambda k: send(SUM_Z, zs.at[0], zs.at[k], z_peer(k)))
    arrived(SUM_Z, zs.at[pl.ds(1, ZS - 1)])
    v = zs[lax.rem(z, ZS)]
    for k in range(1, ZS):
        v = v + zs[lax.rem(z - k + ZS, ZS)]
    fr[0] = v
    each(32, lambda p: send(SPREAD, fr.at[0], fr.at[p], plane_peer(p)))
    arrived(SPREAD, fr.at[pl.ds(1, 31)])

    def place(p, carry):
        q, k = p // HEADS, p % HEADS
        quad = lax.rem(yl + q // 2, 2) * 2 + lax.rem(core + q % 2, 2)
        at = (quad * HEADS + lax.rem(n - k + HEADS, HEADS)) * 16
        flat[pl.ds(pl.multiple_of(at, 16), 16), :] = fr[p]
        return carry
    lax.fori_loop(0, 32, place, 0)
    for j in range(6):
        for m in range(3):
            at = j * 81 + m * 27
            gw_ref[m, :, j * 128:(j + 1) * 128] = flat[at:at + 27, :]
    gg_ref[...] = flat[486:489, 0:HD]

    sent(A2A_P, rb.at[pl.ds(1, HEADS - 1)])
    sent(A2A_G, gr.at[pl.ds(1, HEADS - 1)])
    for stage, span in zip((FWD_ROW, FWD_FRAME, FWD_CORNER), spans):
        sent(stage, hr.at[span])
    sent(GATHER, kvg.at[pl.ds(1, ZS - 1)])
    sent(QUAD, qgr.at[pl.ds(1, 3)])
    sent(STATS, st.at[pl.ds(1, 3)])
    sent(DQ, dqr.at[pl.ds(1, 3)])
    sent(SCATTER, zr.at[pl.ds(1, ZS - 1)])
    for stage, span in zip((BWD_ROW, BWD_FRAME, BWD_CORNER), spans):
        sent(stage, hbr.at[span])
    sent(A2A_B, rb2.at[pl.ds(1, HEADS - 1)])
    sent(SUM_PLANE, kr.at[pl.ds(1, 31)])
    sent(SUM_Z, zs.at[pl.ds(1, ZS - 1)])
    sent(SPREAD, fr.at[pl.ds(1, 31)])


def shards(qkv_fine, grad_out, pool_weight, norm_gain):
    x = qkv_fine[0].transpose(0, 1, 3, 2, 4)
    w = pool_weight.transpose(1, 0, 2).astype(F32)
    vmem = pl.BlockSpec(memory_space=pltpu.VMEM)
    scratch = [
        ((4, 9, 8, 768), F32),
        ((8, 104, 128), F32),
        ((8, 16, 128), BF16),
        ((8, 104, 128), F32),
        ((8, 16, 128), BF16),
        ((416, 128), F32),
        ((256, 128), BF16),
        ((256, 128), BF16),
        ((3, 160, 128), F32),
        ((ZS, 32, 128), BF16),
        ((4, 256, 128), BF16),
        ((256, 512), F32),
        ((256, 512), F32),
        ((4, 8, 128), F32),
        ((4, 128, 128), F32),
        ((4, 128, 128), F32),
        ((ZS, 32, 128), BF16),
        ((ZS, 32, 128), BF16),
        ((256, 128), BF16),
        ((256, 128), BF16),
        ((416, 128), F32),
        ((8, 112, 128), BF16),
        ((8, 112, 128), BF16),
        ((112, 768), BF16),
        ((208, 768), F32),
        ((4, 9, 8, 768), F32),
        ((512, 128), F32),
        ((32, 16, 128), F32),
        ((ZS, 16, 128), F32),
        ((32, 16, 128), F32),
        ((512, 128), F32),
        ((8, 128), F32),
    ]
    gx, gw, gg = pl.pallas_call(
        kernel,
        out_shape=(jax.ShapeDtypeStruct(x.shape, BF16), jax.ShapeDtypeStruct(w.shape, F32),
                   jax.ShapeDtypeStruct(norm_gain.shape, F32)),
        in_specs=[vmem] * 4,
        out_specs=(vmem,) * 3,
        scratch_shapes=[pltpu.VMEM(shape, kind) for shape, kind in scratch]
        + [pltpu.SemaphoreType.DMA((17,)), pltpu.SemaphoreType.DMA((17,))],
        compiler_params=pltpu.CompilerParams(collective_id=0, has_side_effects=True,
                                             vmem_limit_bytes=48 * 1024 * 1024),
    )(x, grad_out[0], w, norm_gain)
    return gx.transpose(0, 1, 3, 2, 4)[None], gw.transpose(1, 0, 2), gg


def solution(mesh):
    in_specs = (P("seq", None, None, "head", None, None), P("seq", None, None, "head", None), P(), P())
    out_specs = (P("seq", None, None, "head", None, None), P(), P())
    return jax.shard_map(shards, mesh=mesh, in_specs=in_specs, out_specs=out_specs, check_vma=False)
```

time: 1260 us -> 102 us (0.08)
  waiting for transfers between devices: 815 us -> 0 us
  blocking collectives: 254 us -> 0 us
  Pallas kernels: 0 us -> 97.3 us
  local copies, waits for them, and re-layouts: 99.1 us -> 3.18 us
  starting transfers between devices: 44.1 us -> 0 us
  other arithmetic: 26.8 us -> 0.94 us
  between operations: 18.1 us -> 0.68 us
    unnamed x3 -> x0, waiting for transfers between devices: 419 us -> none
    psum x1 -> x0, waiting for transfers between devices: 352 us -> none  [shards(): grad_weight, grad_gain = lax.psum((grad_weight, grad_gain), ('seq', 'head'))]
    all_gather x2 -> x0, blocking collectives: 145 us -> none  [the longest x1 82.5 us: attend(): lax.all_gather(key_part, 'seq', axis=0, tiled=True)]
    psum x1 -> x0, blocking collectives: 109 us -> none  [shards(): grad_weight, grad_gain = lax.psum((grad_weight, grad_gain), ('seq', 'head'))]
    pallas_call x0 -> x1, Pallas kernels: none -> 97.3 us  [shards(): pl.pallas_call(kernel, out_shape=(jax.ShapeDtypeStruct(x.shape, BF16), ja...]
    unnamed x334 -> x9, local copies, waits for them, and re-layouts: 57 us -> 3.18 us
    ppermute x4 -> x0, waiting for transfers between devices: 41.8 us -> none  [from_behind(): return lax.ppermute(block, axis, route)]
    ppermute x4 -> x0, starting transfers between devices: 26 us -> none  [from_behind(): return lax.ppermute(block, axis, route)]
  transfers between devices with their start and end apart: 9 -> 0, of which waited for: 6 -> 0; matrix products, arithmetic and copies ran while one was open for 4% -> 0% of each run, Pallas kernels for 0% -> 0%
where the time goes in v1:
time: 102 us
  Pallas kernels  97.3 us (95%)
  local copies, waits for them, and re-layouts  3.18 us (3%)
    pallas_call x1, Pallas kernels, shards(): pl.pallas_call(kernel, out_shape=(jax.ShapeDtypeStruct(x.shape, BF16), ja...  97.3 us
    unnamed x9, local copies, waits for them, and re-layouts  3.18 us

profile of v1, /device:TPU:1, one launch (start us, length us, event | category | flops | bytes accessed | tf_op | source)
XLA Modules:
  0.0 102.1 jit_solution(4484401369827954990)
XLA Ops:
  0.6 0.0 copy-start.1
  0.6 0.0 copy-start.2
  0.7 0.9 convert_bitcast_fusion.w_ref
  1.6 0.0 copy-done.1
  1.6 0.0 copy-done.2
  1.6 0.0 copy-start
  1.6 1.1 %copy-done = bf16[1,4,4,8,3,768]{5,3,4,2,1,0:T(8,128)(2,1)S(1)} copy-done((bf16[1,4,4,8,3,768]{5,3,4,2,1,0:T(8,128)(2,1)S(1)}, bf16[1,4,4,8,3,768]{5,3,4,2,1,0:T(8,128)(2,1)}, u32[]{:S(2)}) %copy-start) | copy-done | bytes 589848
  2.7 97.3 %shard_map.67 = (bf16[4,4,3,8,768]{4,3,2,1,0:T(8,128)(2,1)S(1)}, f32[3,27,768]{2,1,0:T(8,128)S(1)}, f32[3,96]{1,0:T(4,128)S(1)}) custom-call(bf16[4,4,3,8,768]{4,3,2,1,0:T(8,128)(2,1)S(1)} %bitcast.10, bf16[2,2,4,768]{3,2,1,0:T(4,128)(2,1)S(1)} %bitcast.13, f32[3,27,768]{2,1,0:T(8,128)S(1)} %convert_bitcast_fusion.w_ref, f32[3,96]{1,0:T(4,128)S(1)} %copy-done.2), custom_call_target="tpu_custom_call" | custom-call | tf_op jit(solution)/shard_map/pallas_call | solution.py:544
  99.9 0.8 copy.10
  100.8 0.7 copy.11
  101.5 0.6 copy.12
Async XLA Ops:
  0.6 1.0 copy-start.1
  0.6 1.0 copy-start.2
  1.6 1.1 %copy-start = (bf16[1,4,4,8,3,768]{5,3,4,2,1,0:T(8,128)(2,1)S(1)}, bf16[1,4,4,8,3,768]{5,3,4,2,1,0:T(8,128)(2,1)}, u32[]{:S(2)}) copy-start(bf16[1,4,4,8,3,768]{5,3,4,2,1,0:T(8,128)(2,1)} %param.4) | copy-start | bytes 1769476

commit v2 on v1

v2 whole, which is shorter than its diff:
```python
import jax
import jax.numpy as jnp
from jax import lax
from jax.experimental import pallas as pl
from jax.experimental.pallas import tpu as pltpu
from jax.sharding import PartitionSpec as P

MESH = pl.DeviceIdType.MESH
F32 = jnp.float32
BF16 = jnp.bfloat16
HD = 96
HEADS = 8
ROW_GROUPS = 16
SEQ = 64
ZS = 16
SCALE = HD ** -0.5

PAIRS_Q = (((0, 1), (1, 2)), ((1, 0), (2, 1), (3, 2)), ((3, 0),))
PAIRS_K = (((0, 1), (1, 2)), ((3, 0),))
OWN_Q = (0, 1, 3, 4)

(A2A_F, FINE, KV_ROW, KV_FRAME, KV_CORNER, Q_ROW, Q_FRAME, Q_CORNER, GATHER, QUAD, STATS, DQ, SCATTER, BQ_ROW, BQ_FRAME,
 BQ_CORNER, BK_ROW, BK_FRAME, BK_CORNER, A2A_B, SUM_QUAD, SUM_Z, SPREAD) = range(23)
FAR_FIRST = (8, 7, 9, 6, 10, 5, 11, 4, 12, 3, 13, 2, 14, 1, 15)
KV_SPANS = ((0, 32), (32, 32), (64, 32))
Q_SPANS = ((96, 64), (160, 64), (224, 32))


def iota(shape, dim):
    return lax.broadcasted_iota(jnp.int32, shape, dim)


def up(x, by):
    size = x.shape[0]
    return pltpu.roll(x, (size - by) % size, 0)


def split_heads(tiles):
    lane = iota(tiles[0].shape, 1)
    heads = []
    for n in range(HEADS):
        t = tiles[n // 4 * 3:n // 4 * 3 + 3]
        if n % 4 == 0:
            v = t[0]
        elif n % 4 == 1:
            v = jnp.where(lane < 32, pltpu.roll(t[0], 32, 1), pltpu.roll(t[1], 32, 1))
        elif n % 4 == 2:
            v = jnp.where(lane < 64, pltpu.roll(t[1], 64, 1), pltpu.roll(t[2], 64, 1))
        else:
            v = pltpu.roll(t[2], 96, 1)
        heads.append(jnp.where(lane < HD, v, 0.0))
    return heads


def merge_heads(h):
    lane = iota(h[0].shape, 1)
    tiles = []
    for half in (0, 4):
        a, b, c, d = h[half:half + 4]
        tiles.append(jnp.where(lane < 96, a, pltpu.roll(b, 96, 1)))
        tiles.append(jnp.where(lane < 64, pltpu.roll(b, 96, 1), pltpu.roll(c, 64, 1)))
        tiles.append(jnp.where(lane < 32, pltpu.roll(c, 64, 1), pltpu.roll(d, 32, 1)))
    return tiles


def tiles_of(v):
    return [v[:, j * 128:(j + 1) * 128] for j in range(6)]


def kernel(x_ref, g_ref, w_ref, gain_ref, gx_ref, gw_ref, gg_ref,
           xv, wf, wt, sb, rb, xs, xr, xf, pe, hs, hr, norm, kvg, qgr, raised_ref, ga_ref, st, dqb, dqr, zb, zr,
           hb, hbr, ge, exh, sb2, rb2, gall, ex, gxv, wg, wb, kr, zs, fr, flat, gsc, ss, rs, local):
    s = lax.axis_index("seq")
    n = lax.axis_index("head")
    group, u = s // ROW_GROUPS, s % ROW_GROUPS
    yl, z, core = s // (2 * ZS), s // 2 % ZS, s % 2

    load = pltpu.make_async_copy(x_ref, xv, local.at[0])
    load.start()

    def head_peer(k):
        return (s, lax.rem(n + k, HEADS))

    def z_peer(k):
        return (yl * (2 * ZS) + lax.rem(z + k, ZS) * 2 + core, n)

    def quad_peer(k):
        return (lax.rem(yl + k // 2, 2) * (2 * ZS) + z * 2 + lax.rem(core + k % 2, 2), n)

    def quad_index(k):
        return lax.rem(yl + k // 2, 2) * 2 + lax.rem(core + k % 2, 2)

    def plane_peer(p):
        return (quad_peer(p // HEADS)[0], lax.rem(n + p % HEADS, HEADS))

    def seq_peer(d):
        return (lax.rem(s + d + SEQ, SEQ), n)

    barrier = pltpu.get_barrier_semaphore()
    greeted = [seq_peer(d) for d in (16, 17, -16, -17)] + [z_peer(k) for k in FAR_FIRST]
    greeted += [seq_peer(1), seq_peer(-1)] + [quad_peer(k) for k in (3, 2, 1)] + [head_peer(k) for k in range(1, HEADS)]
    for peer in greeted:
        pl.semaphore_signal(barrier, inc=1, device_id=peer, device_id_type=MESH)

    def send(stage, src, dst, peer):
        pltpu.make_async_remote_copy(src_ref=src, dst_ref=dst, send_sem=ss.at[stage], recv_sem=rs.at[stage],
                                     device_id=peer, device_id_type=MESH).start()

    def arrived(stage, ref):
        pltpu.make_async_copy(ref, ref, rs.at[stage]).wait()

    pending = []

    def drain():
        for stage, ref in pending:
            pltpu.make_async_copy(ref, ref, ss.at[stage]).wait()

    row = iota((8, 768), 0)
    row8 = iota((8, 128), 0)
    lane8 = iota((8, 128), 1)
    wf[...] = w_ref[...].astype(F32)

    def taps(ab, carry):
        def one(m, e):
            return jnp.broadcast_to(wf[m, pl.ds(ab * 3 + e, 1), :], (8, 768))
        wt[0, ab] = jnp.where(row % 2 == 0, one(0, 1), one(0, 2))
        wt[1, ab] = jnp.where(row % 2 == 1, one(0, 0), 0.0)
        for m in (1, 2):
            wt[1 + m, ab] = jnp.where(row % 4 == 0, one(m, 1), jnp.where(
                row % 4 == 1, one(m, 2), jnp.where(row % 4 == 3, one(m, 0), 0.0)))
        return carry
    lax.fori_loop(0, 9, taps, 0)
    gsc[...] = jnp.zeros_like(gsc)
    gsc[0:3, 0:HD] = gain_ref[...]
    load.wait()

    def fine(m, f, r):
        return xv[(f * 4 + r) * 3 + m].astype(F32)

    groups = []
    for t in range(3):
        for y in range(3):
            a_sum = b_sum = None
            for f, a in PAIRS_Q[t]:
                for r, b in PAIRS_Q[y]:
                    v = fine(0, f, r)
                    ta, tb = v * wt[0, a * 3 + b], v * wt[1, a * 3 + b]
                    a_sum = ta if a_sum is None else a_sum + ta
                    b_sum = tb if b_sum is None else b_sum + tb
            b1 = pltpu.roll(b_sum, 1, 0)
            e = a_sum + up(a_sum, 1) + jnp.where(row == 0, 0.0, b1)
            v = jnp.where(row == 0, e, jnp.where(row == 1, up(e, 1), jnp.where(row == 2, up(e, 2), jnp.where(
                row == 3, up(e, 3), jnp.where(row == 4, up(b1, 4), 0.0)))))
            groups.append(v)
    for t in range(2):
        for y in range(2):
            both = []
            for m in (1, 2):
                k_sum = None
                for f, a in PAIRS_K[t]:
                    for r, b in PAIRS_K[y]:
                        tk = fine(m, f, r) * wt[1 + m, a * 3 + b]
                        k_sum = tk if k_sum is None else k_sum + tk
                t1 = k_sum + up(k_sum, 1)
                both.append(jnp.where(row == 0, t1, jnp.where(row == 1, up(t1, 2) + up(k_sum, 4), jnp.where(
                    row == 2, up(k_sum, 5), 0.0))))
            groups.append(both[0] + pltpu.roll(both[1], 4, 0))
    groups.append(jnp.zeros((8, 768), F32))
    for t in range(2):
        groups.append(jnp.concatenate([g_ref[t, 0].astype(F32), g_ref[t, 1].astype(F32)], 0))
    for p in range(8):
        v = jnp.concatenate(groups[2 * p:2 * p + 2], 0)
        for h, part in enumerate(split_heads(tiles_of(v))):
            sb[h, p * 16:p * 16 + 16, :] = part.astype(BF16)

    pl.semaphore_wait(barrier, len(greeted))
    for k in range(1, HEADS):
        peer = head_peer(k)
        send(A2A_F, sb.at[peer[1]], rb.at[k], peer)
    pending.append((A2A_F, rb.at[pl.ds(1, HEADS - 1)]))
    rb[0] = sb[n]

    def split_fine(p, carry):
        v = jnp.concatenate([xv[2 * p].astype(F32), xv[2 * p + 1].astype(F32)], 0)
        for h, part in enumerate(split_heads(tiles_of(v))):
            xs[h, pl.ds(pl.multiple_of(p * 16, 16), 16), :] = part.astype(BF16)
        return carry
    lax.fori_loop(0, 24, split_fine, 0)
    arrived(A2A_F, rb.at[pl.ds(1, HEADS - 1)])

    from_col = [lax.rem(n - h + HEADS, HEADS) for h in range(HEADS)]
    sets = [rb[from_col[h]].astype(F32) for h in range(HEADS)]
    for grp in range(4):
        parts = [v[72 + grp * 8:80 + grp * 8] for v in sets]
        for m in range(2):
            if m == 0:
                own = [jnp.where(row8 < 4, p, 0.0) for p in parts]
            else:
                own = [pltpu.roll(jnp.where(row8 >= 4, p, 0.0), 4, 0) for p in parts]
            last = [pltpu.roll(own[4 * j + 3], 6, 0) for j in range(2)]
            for j in range(2):
                v = own[4 * j] + pltpu.roll(own[4 * j + 1], 2, 0) + pltpu.roll(own[4 * j + 2], 4, 0)
                v = v + jnp.where(row8 >= 4, last[j], 0.0)
                if j:
                    v = v + jnp.where(row8 == 0, last[0], 0.0)
                at = 288 + m * 64 + grp * 16 + j * 8
                pe[at:at + 8, :] = v

    def pq(t, y):
        return pe[(t * 3 + y) * 32:(t * 3 + y) * 32 + 32, :]

    def pkv(t, y):
        at = 288 + (t * 2 + y) * 16
        return jnp.concatenate([pe[at:at + 16, :], pe[at + 64:at + 80, :]], 0)

    def exchange(stages, spans, src, dst, distances):
        for stage, (lo, count), d in zip(stages, spans, distances):
            send(stage, src.at[pl.ds(lo, count)], dst.at[pl.ds(lo, count)], seq_peer(d))
            pending.append((stage, dst.at[pl.ds(lo, count)]))

    def exchanged(stages, spans, dst):
        for stage, (lo, count) in zip(stages, spans):
            arrived(stage, dst.at[pl.ds(lo, count)])

    hs[0:96, :] = jnp.concatenate([pkv(0, 1), pkv(1, 0), pkv(1, 1)], 0).astype(BF16)
    exchange((KV_ROW, KV_FRAME, KV_CORNER), KV_SPANS, hs, hr, (1, 16, 17))
    for grp in range(9):
        parts = [v[grp * 8:grp * 8 + 8] for v in sets]
        rolled = [pltpu.roll(parts[2 * j + 1], 4, 0) for j in range(4)]
        for j in range(4):
            v = parts[2 * j] + jnp.where(row8 >= 4, rolled[j], 0.0)
            if j:
                v = v + jnp.where(row8 == 0, rolled[j - 1], 0.0)
            pe[grp * 32 + j * 8:grp * 32 + j * 8 + 8, :] = v
    hs[96:256, :] = jnp.concatenate([pq(0, 2), pq(1, 2), pq(2, 0), pq(2, 1), pq(2, 2)], 0).astype(BF16)
    exchange((Q_ROW, Q_FRAME, Q_CORNER), Q_SPANS, hs, hr, (1, 16, 17))
    for k in range(1, HEADS):
        peer = head_peer(k)
        send(FINE, xs.at[peer[1]], xr.at[k], peer)
    pending.append((FINE, xr.at[pl.ds(1, HEADS - 1)]))
    xr[0] = xs[n]

    for t in range(2):
        for y in range(2):
            vs = []
            for j in range(4):
                a, b = (sets[2 * j + i][112 + t * 8:120 + t * 8] for i in range(2))
                if y == 0:
                    vs.append(jnp.where(row8 < 4, a, pltpu.roll(b, 4, 0)))
                else:
                    vs.append(jnp.where(row8 < 4, pltpu.roll(a, 4, 0), b))
            at = 128 + (t * 2 + y) * 32
            qgr[0, at:at + 32, :] = jnp.concatenate(vs, 0).astype(BF16)

    def layer_norm(pooled, lo, count, gain):
        lane = iota((count, 128), 1)
        centred = jnp.where(lane < HD, pooled - jnp.sum(pooled, 1, keepdims=True) * (1.0 / HD), 0.0)
        rstd = lax.rsqrt(jnp.sum(centred * centred, 1, keepdims=True) * (1.0 / HD) + 1e-6)
        unit = centred * rstd
        norm[0, lo:lo + count, :] = unit
        norm[1, lo:lo + count, :] = jnp.broadcast_to(rstd, (count, 128))
        return (unit * gain).astype(BF16)

    has_u = (u > 0).astype(F32)
    has_g = (group > 0).astype(F32)
    has_c = has_u * has_g

    def border(lo, count, has):
        return hr[lo:lo + count, :].astype(F32) * has

    exchanged((KV_ROW, KV_FRAME, KV_CORNER), KV_SPANS, hr)
    gain_kv = jnp.where(iota((32, 128), 0) < 16, gsc[1:2, :], gsc[2:3, :])
    gain_q = jnp.broadcast_to(gsc[0:1, :], (128, 128))
    kvg[0] = layer_norm(pkv(0, 0) + border(0, 32, has_u) + border(32, 32, has_g) + border(64, 32, has_c), 128, 32, gain_kv)
    for k in FAR_FIRST:
        send(GATHER, kvg.at[0], kvg.at[k], z_peer(k))
    pending.append((GATHER, kvg.at[pl.ds(1, ZS - 1)]))

    exchanged((Q_ROW, Q_FRAME, Q_CORNER), Q_SPANS, hr)
    q00 = pq(0, 0) + border(96, 32, has_u) + border(160, 32, has_g) + border(224, 32, has_c)
    q01 = pq(0, 1) + border(192, 32, has_g)
    q10 = pq(1, 0) + border(128, 32, has_u)
    qgr[0, 0:128, :] = layer_norm(jnp.concatenate([q00, q01, q10, pq(1, 1)], 0), 0, 128, gain_q)
    for k in (2, 3, 1):
        send(QUAD, qgr.at[0], qgr.at[k], quad_peer(k))
    pending.append((QUAD, qgr.at[pl.ds(1, 3)]))
    arrived(QUAD, qgr.at[pl.ds(1, 3)])
    arrived(GATHER, kvg.at[pl.ds(1, ZS - 1)])

    keys = kvg[:, 0:16, :].reshape(256, 128)
    values = kvg[:, 16:32, :].reshape(256, 128)
    queries = qgr[:, 0:128, :].reshape(512, 128)
    grads = qgr[:, 128:256, :].reshape(512, 128)
    nt = (((1,), (1,)), ((), ()))
    raised_ref[...] = jnp.exp(lax.dot_general(keys, queries, nt, preferred_element_type=F32) * SCALE)
    ga_ref[...] = lax.dot_general(values, grads, nt, preferred_element_type=F32)
    total = jnp.sum(raised_ref[...], 0, keepdims=True)
    delta = jnp.sum(raised_ref[...] * ga_ref[...], 0, keepdims=True)
    for j in range(4):
        st[0, j:j + 1, :] = total[:, j * 128:(j + 1) * 128]
        st[0, 4 + j:5 + j, :] = delta[:, j * 128:(j + 1) * 128]
    for k in (2, 3, 1):
        send(STATS, st.at[0], st.at[k], quad_peer(k))
    pending.append((STATS, st.at[pl.ds(1, 3)]))
    arrived(STATS, st.at[pl.ds(1, 3)])

    def quad_sum(at):
        outs = []
        for j in range(4):
            v = st[0, at + j:at + j + 1, :]
            for k in range(1, 4):
                i = at + (j ^ k)
                v = v + st[k, i:i + 1, :]
            outs.append(v)
        return jnp.concatenate(outs, 1)

    inverse = 1.0 / quad_sum(0)
    row_delta = quad_sum(4) * inverse
    attention = raised_ref[...] * inverse
    grad_scores = (attention * (ga_ref[...] - row_delta)).astype(BF16)
    grad_key = jnp.dot(grad_scores, queries, preferred_element_type=F32) * SCALE
    grad_value = jnp.dot(attention.astype(BF16), grads, preferred_element_type=F32)
    zb[:, 0:16, :] = grad_key.reshape(ZS, 16, 128).astype(BF16)
    zb[:, 16:32, :] = grad_value.reshape(ZS, 16, 128).astype(BF16)
    for k in FAR_FIRST:
        send(SCATTER, zb.at[k], zr.at[k], z_peer(ZS - k))
    pending.append((SCATTER, zr.at[pl.ds(1, ZS - 1)]))
    grad_query = lax.dot_general(grad_scores, keys, (((0,), (0,)), ((), ())), preferred_element_type=F32)
    dqb[...] = grad_query.reshape(4, 128, 128)
    for k in (2, 3, 1):
        send(DQ, dqb.at[k], dqr.at[k], quad_peer(k))
    pending.append((DQ, dqr.at[pl.ds(1, 3)]))
    zr[0] = zb[0]
    dqr[0] = dqb[0]

    def norm_backward(grad_normed, lo, count, gain):
        lane = iota((count, 128), 1)
        unit = norm[0, lo:lo + count, :]
        inner = grad_normed * gain
        mean_1 = jnp.sum(inner, 1, keepdims=True) * (1.0 / HD)
        mean_2 = jnp.sum(inner * unit, 1, keepdims=True) * (1.0 / HD)
        out = norm[1, lo:lo + count, :] * jnp.where(lane < HD, inner - mean_1 - unit * mean_2, 0.0)
        return out, grad_normed * unit

    arrived(DQ, dqr.at[pl.ds(1, 3)])
    dq = dqr[0] + dqr[1] + dqr[2] + dqr[3]
    gq, gain_rows = norm_backward(dq * SCALE + qgr[0, 128:256, :].astype(F32), 0, 128, gain_q)
    wg[80:88, :] = jnp.zeros((8, 128), F32)
    wg[81:82, :] = jnp.sum(gain_rows, 0, keepdims=True)
    hb[96:256, :] = jnp.concatenate([gq[0:32], gq[64:96], gq[0:64], gq[0:32]], 0).astype(BF16)
    exchange((BQ_ROW, BQ_FRAME, BQ_CORNER), Q_SPANS, hb, hbr, (-1, -16, -17))
    for i, grp in enumerate(OWN_Q):
        ge[grp * 32:grp * 32 + 32, :] = gq[i * 32:i * 32 + 32]

    arrived(FINE, xr.at[pl.ds(1, HEADS - 1)])
    for h in range(HEADS):
        xf[:, h * 8:h * 8 + 8, :] = xr[from_col[h]].astype(F32).reshape(48, 8, 128)

    arrived(SCATTER, zr.at[pl.ds(1, ZS - 1)])
    gkv, gain_rows = norm_backward(jnp.sum(zr[...].astype(F32), 0), 128, 32, gain_kv)
    wg[82:83, :] = jnp.sum(gain_rows[0:16], 0, keepdims=True)
    wg[83:84, :] = jnp.sum(gain_rows[16:32], 0, keepdims=True)
    hb[0:96, :] = jnp.concatenate([gkv, gkv, gkv], 0).astype(BF16)
    exchange((BK_ROW, BK_FRAME, BK_CORNER), KV_SPANS, hb, hbr, (-1, -16, -17))
    ge[288:304, :] = gkv[0:16]
    ge[352:368, :] = gkv[16:32]
    back_u = (u < ROW_GROUPS - 1).astype(F32)
    back_g = (group < SEQ // ROW_GROUPS - 1).astype(F32)
    back_c = back_u * back_g

    def returned(lo, count, has):
        return hbr[lo:lo + count, :].astype(F32) * has

    exchanged((BQ_ROW, BQ_FRAME, BQ_CORNER), Q_SPANS, hbr)
    ge[2 * 32:3 * 32, :] = returned(96, 32, back_u)
    ge[5 * 32:6 * 32, :] = returned(128, 32, back_u)
    ge[6 * 32:8 * 32, :] = returned(160, 64, back_g)
    ge[8 * 32:9 * 32, :] = returned(224, 32, back_c)

    def pairs(pair_list, a):
        return [(f, t) for t, entries in enumerate(pair_list) for f, tap in entries if tap == a]

    def spread(rows, cols, target):
        return jnp.where(iota((rows, cols), 1) == target, 1.0, 0.0).astype(BF16)

    r = iota((128, 32), 0)
    spread_q = spread(128, 32, ((r & 63) >> 1) + (r >> 6))
    spread_k = spread(64, 16, (iota((64, 16), 0) + 1) >> 2)
    row64 = iota((64, 128), 0)
    for grp in range(9):
        exh[grp * 128:grp * 128 + 128, :] = jnp.dot(spread_q, ge[grp * 32:grp * 32 + 32, :].astype(BF16),
                                                    preferred_element_type=F32)

    def tap_rows(masked, m, ab):
        for e, v in enumerate(masked):
            wg[m * 27 + ab * 3 + e:m * 27 + ab * 3 + e + 1, :] = jnp.sum(v, 0, keepdims=True)

    for a in range(3):
        for b in range(3):
            first = second = None
            for f, t in pairs(PAIRS_Q, a):
                for rr, y in pairs(PAIRS_Q, b):
                    v, at = xf[(f * 4 + rr) * 3], (t * 3 + y) * 128
                    t1, t2 = v * exh[at:at + 64, :], v * exh[at + 64:at + 128, :]
                    first = t1 if first is None else first + t1
                    second = t2 if second is None else second + t2
            tap_rows((jnp.where(row64 % 2 == 1, second, 0.0), jnp.where(row64 % 2 == 0, first, 0.0),
                      jnp.where(row64 % 2 == 1, first, 0.0)), 0, a * 3 + b)

    exchanged((BK_ROW, BK_FRAME, BK_CORNER), KV_SPANS, hbr)
    for lo, at, has in ((0, 16, back_u), (32, 32, back_g), (64, 48, back_c)):
        v = returned(lo, 32, has)
        ge[288 + at:304 + at, :] = v[0:16]
        ge[352 + at:368 + at, :] = v[16:32]
    for m in (1, 2):
        wide = [jnp.dot(spread_k, ge[at:at + 16, :].astype(BF16), preferred_element_type=F32)
                for at in range(224 + m * 64, 288 + m * 64, 16)]
        for a in range(3):
            for b in range(3):
                (f, t), = pairs(PAIRS_K, a)
                (rr, y), = pairs(PAIRS_K, b)
                v = xf[(f * 4 + rr) * 3 + m] * wide[t * 2 + y]
                tap_rows(tuple(jnp.where(row64 % 4 == c, v, 0.0) for c in (3, 0, 1)), m, a * 3 + b)

    t16, t8 = wg[64:80, :], wg[80:88, :]
    tail = jnp.concatenate([pltpu.roll(t16, 96, 1), pltpu.roll(t16, 64, 1), pltpu.roll(t16, 32, 1),
                            jnp.where(row8 < 4, pltpu.roll(t8, 96, 1), pltpu.roll(pltpu.roll(t8, 64, 1), 4, 0)),
                            pltpu.roll(t8, 32, 1)], 0)
    wb[...] = jnp.where(iota((64, 128), 1) < HD, wg[0:64, :], tail)

    def piece(k):
        return pl.ds(pl.multiple_of(quad_index(k) * 16, 16), 16)

    for k in (2, 3, 1):
        send(SUM_QUAD, wb.at[piece(k)], kr.at[k], quad_peer(k))
    pending.append((SUM_QUAD, kr.at[pl.ds(1, 3)]))
    kr[0] = wb[piece(0), :]

    zero = jnp.zeros((8, 128), F32)
    out_rows = [[] for _ in range(HEADS)]
    for grp in range(9):
        vs = [ge[grp * 32 + j * 8:grp * 32 + j * 8 + 8, :] for j in range(4)] + [zero]
        half = [pltpu.roll(v, 4, 0) for v in vs]
        for h in range(HEADS):
            j = h // 2
            out_rows[h].append(vs[j] if h % 2 == 0 else jnp.where(row8 < 4, half[j], half[j + 1]))
    for grp in range(4):
        vs = [[ge[at:at + 8, :] for at in (288 + m * 64 + grp * 16, 296 + m * 64 + grp * 16)] + [zero] for m in range(2)]
        for h in range(HEADS):
            j, i = h // 4, h % 4
            parts = []
            for m in range(2):
                v = pltpu.roll(vs[m][j], 8 - 2 * i, 0) if i else vs[m][j]
                if i == 3:
                    v = jnp.where(row8 < 2, v, pltpu.roll(vs[m][j + 1], 2, 0))
                parts.append(v)
            out_rows[h].append(jnp.where(row8 < 4, parts[0], pltpu.roll(parts[1], 4, 0)))
    for h in range(HEADS):
        sb2[h] = jnp.concatenate(out_rows[h] + [zero], 0).astype(BF16)
    for k in range(1, HEADS):
        peer = head_peer(k)
        send(A2A_B, sb2.at[peer[1]], rb2.at[k], peer)
    pending.append((A2A_B, rb2.at[pl.ds(1, HEADS - 1)]))
    rb2[0] = sb2[n]

    arrived(SUM_QUAD, kr.at[pl.ds(1, 3)])
    zs[0] = (kr[0] + kr[1] + kr[2] + kr[3]).astype(zs.dtype)
    for k in FAR_FIRST:
        send(SUM_Z, zs.at[0], zs.at[k], z_peer(k))
    pending.append((SUM_Z, zs.at[pl.ds(1, ZS - 1)]))

    arrived(A2A_B, rb2.at[pl.ds(1, HEADS - 1)])
    tiles = merge_heads([rb2[from_col[h]].astype(F32) for h in range(HEADS)])
    for j in range(6):
        gall[:, j * 128:(j + 1) * 128] = tiles[j].astype(BF16)
    r = iota((208, 112), 0)
    grp, late, i = r >> 4, (r >> 3) & 1, r & 7
    ex[...] = jnp.dot(spread(208, 112, grp * 8 + jnp.where(grp < 9, (i >> 1) + late, ((i + 1) >> 2) + 4 * late)),
                      gall[...], preferred_element_type=F32)

    def g_at(grp, late):
        at = grp * 16 + late * 8
        return ex[at:at + 8, :]

    def reached(pair_list, f):
        return [(t, a) for t, entries in enumerate(pair_list) for ff, a in entries if ff == f]

    for f in range(4):
        for rr in range(4):
            q_sum = None
            for t, a in reached(PAIRS_Q, f):
                for y, b in reached(PAIRS_Q, rr):
                    term = g_at(t * 3 + y, 0) * wt[0, a * 3 + b] + g_at(t * 3 + y, 1) * wt[1, a * 3 + b]
                    q_sum = term if q_sum is None else q_sum + term
            gxv[(f * 4 + rr) * 3] = q_sum.astype(BF16)
            for m in (1, 2):
                k_sum = jnp.zeros((8, 768), F32)
                for t, a in reached(PAIRS_K, f):
                    for y, b in reached(PAIRS_K, rr):
                        k_sum = g_at(9 + t * 2 + y, m - 1) * wt[1 + m, a * 3 + b]
                gxv[(f * 4 + rr) * 3 + m] = k_sum.astype(BF16)
    store = pltpu.make_async_copy(gxv, gx_ref, local.at[1])
    store.start()

    arrived(SUM_Z, zs.at[pl.ds(1, ZS - 1)])
    v = zs[z].astype(F32)
    for k in range(1, ZS):
        v = v + zs[lax.rem(z - k + ZS, ZS)].astype(F32)
    fr[0] = v
    for p in range(31, 0, -1):
        send(SPREAD, fr.at[0], fr.at[p], plane_peer(p))
    pending.append((SPREAD, fr.at[pl.ds(1, 31)]))
    arrived(SPREAD, fr.at[pl.ds(1, 31)])

    lane16 = iota((16, 128), 1)
    unpacked, gains = [], None
    for h in range(HEADS):
        at = [fr[lax.rem(yl + q // 2, 2) * (2 * HEADS) + lax.rem(core + q % 2, 2) * HEADS + from_col[h]] for q in range(4)]
        t16 = jnp.where(lane16 < 32, pltpu.roll(at[0], 32, 1), jnp.where(
            lane16 < 64, pltpu.roll(at[1], 64, 1), pltpu.roll(at[2], 96, 1)))
        lo, hi = at[3][0:8], at[3][8:16]
        t8 = jnp.where(lane8 < 32, pltpu.roll(lo, 32, 1), jnp.where(
            lane8 < 64, pltpu.roll(pltpu.roll(lo, 64, 1), 4, 0), pltpu.roll(hi, 96, 1)))
        gains = t8 if gains is None else gains + t8
        unpacked.append(jnp.concatenate(at + [t16, t8], 0))
    for j, v in enumerate(merge_heads(unpacked)):
        flat[j * 88:j * 88 + 88, :] = v
    for j in range(6):
        for m in range(3):
            gw_ref[m, :, j * 128:(j + 1) * 128] = flat[j * 88 + m * 27:j * 88 + m * 27 + 27, :]
    gg_ref[...] = gains[1:4, 0:HD]
    store.wait()
    drain()


def shards(qkv_fine, grad_out, pool_weight, norm_gain):
    x = qkv_fine[0].transpose(0, 1, 3, 2, 4).reshape(48, 8, 768)
    w = pool_weight.transpose(1, 0, 2)
    vmem = pl.BlockSpec(memory_space=pltpu.VMEM)
    hbm = pl.BlockSpec(memory_space=pl.ANY)
    scratch = [
        ((48, 8, 768), BF16),
        ((3, 27, 768), F32),
        ((4, 9, 8, 768), F32),
        ((8, 128, 128), BF16),
        ((8, 128, 128), BF16),
        ((8, 384, 128), BF16),
        ((8, 384, 128), BF16),
        ((48, 64, 128), F32),
        ((416, 128), F32),
        ((256, 128), BF16),
        ((256, 128), BF16),
        ((2, 160, 128), F32),
        ((ZS, 32, 128), BF16),
        ((4, 256, 128), BF16),
        ((256, 512), F32),
        ((256, 512), F32),
        ((4, 8, 128), F32),
        ((4, 128, 128), F32),
        ((4, 128, 128), F32),
        ((ZS, 32, 128), BF16),
        ((ZS, 32, 128), BF16),
        ((256, 128), BF16),
        ((256, 128), BF16),
        ((416, 128), F32),
        ((9 * 128, 128), F32),
        ((8, 112, 128), BF16),
        ((8, 112, 128), BF16),
        ((112, 768), BF16),
        ((208, 768), F32),
        ((48, 8, 768), BF16),
        ((88, 128), F32),
        ((64, 128), F32),
        ((4, 16, 128), F32),
        ((ZS, 16, 128), BF16),
        ((32, 16, 128), F32),
        ((6 * 88, 128), F32),
        ((8, 128), F32),
    ]
    gx, gw, gg = pl.pallas_call(
        kernel,
        out_shape=(jax.ShapeDtypeStruct(x.shape, BF16), jax.ShapeDtypeStruct(w.shape, F32),
                   jax.ShapeDtypeStruct(norm_gain.shape, F32)),
        in_specs=[hbm] + [vmem] * 3,
        out_specs=(hbm, vmem, vmem),
        scratch_shapes=[pltpu.VMEM(shape, kind) for shape, kind in scratch]
        + [pltpu.SemaphoreType.DMA((23,)), pltpu.SemaphoreType.DMA((23,)), pltpu.SemaphoreType.DMA((2,))],
        compiler_params=pltpu.CompilerParams(collective_id=0, has_side_effects=True,
                                             vmem_limit_bytes=60 * 1024 * 1024),
    )(x, grad_out[0], w, norm_gain)
    return gx.reshape(4, 4, 3, 8, 768).transpose(0, 1, 3, 2, 4)[None], gw.transpose(1, 0, 2), gg


def solution(mesh):
    in_specs = (P("seq", None, None, "head", None, None), P("seq", None, None, "head", None), P(), P())
    out_specs = (P("seq", None, None, "head", None, None), P(), P())
    return jax.shard_map(shards, mesh=mesh, in_specs=in_specs, out_specs=out_specs, check_vma=False)
```

time: 102 us -> 82.9 us (0.81)
  Pallas kernels: 97.3 us -> 78.7 us
    pallas_call x1, Pallas kernels: 97.3 us -> 78.7 us  [shards(): pl.pallas_call(kernel, out_shape=(jax.ShapeDtypeStruct(x.shape, BF16), ja...]
    unnamed x9 -> x7, local copies, waits for them, and re-layouts: 3.18 us -> 3.26 us
where the time goes in v2:
time: 82.9 us; the launch traced here: 82.6 us
  Pallas kernels  78.7 us (95%)
  local copies, waits for them, and re-layouts  3.26 us (4%)
    pallas_call x1, Pallas kernels, shards(): pl.pallas_call(kernel, out_shape=(jax.ShapeDtypeStruct(x.shape, BF16), ja...  78.7 us
    unnamed x7, local copies, waits for them, and re-layouts  3.26 us

profile of v2, /device:TPU:1, one launch (start us, length us, event | category | flops | bytes accessed | tf_op | source)
XLA Modules:
  0.0 82.6 jit_solution(3297294405954990413)
XLA Ops:
  0.6 78.7 %shard_map.67 = (bf16[48,8,768]{2,1,0:T(8,128)(2,1)}, f32[3,27,768]{2,1,0:T(8,128)}, f32[3,96]{1,0:T(4,128)}) custom-call(bf16[48,8,768]{2,1,0:T(8,128)(2,1)} %bitcast.13, bf16[2,2,4,768]{3,2,1,0:T(4,128)(2,1)} %bitcast.17, bf16[3,27,768]{2,1,0:T(8,128)(2,1)} %bitcast.16, f32[3,96]{1,0:T(4,128)} %gain_ref.1), custom_call_target="tpu_custom_call" | custom-call | tf_op jit(solution)/shard_map/pallas_call | solution.py:580
  79.4 0.0 copy-start
  79.4 2.0 %copy.10 = bf16[1,4,4,8,3,768]{5,3,4,2,1,0:T(8,128)(2,1)} copy(bf16[1,4,4,8,3,768]{5,3,4,2,1,0:T(8,128)(2,1)} %bitcast.14) | data formatting | bytes 1179648
  81.3 0.0 copy-done
  81.4 0.0 copy-start.1
  81.4 0.7 copy.11
  82.1 0.0 copy-done.1
  82.1 0.6 copy.12
Async XLA Ops:
  79.4 2.0 %copy-start = (f32[3,27,768]{2,1,0:T(8,128)S(1)}, f32[3,27,768]{2,1,0:T(8,128)}, u32[]{:S(2)}) copy-start(f32[3,27,768]{2,1,0:T(8,128)} %get-tuple-element.7) | copy-start | bytes 746500
  81.4 0.7 copy-start.1

commit v3 on v2

--- a/solution.py
+++ b/solution.py
@@ -19,8 +19,8 @@
 PAIRS_K = (((0, 1), (1, 2)), ((3, 0),))
 OWN_Q = (0, 1, 3, 4)
 
-(A2A_F, FINE, KV_ROW, KV_FRAME, KV_CORNER, Q_ROW, Q_FRAME, Q_CORNER, GATHER, QUAD, STATS, DQ, SCATTER, BQ_ROW, BQ_FRAME,
- BQ_CORNER, BK_ROW, BK_FRAME, BK_CORNER, A2A_B, SUM_QUAD, SUM_Z, SPREAD) = range(23)
+(A2A_K, A2A_Q, FINE, KV_ROW, KV_FRAME, KV_CORNER, Q_ROW, Q_FRAME, Q_CORNER, GATHER, QUAD, STATS, DQ, SCATTER, BQ_ROW, BQ_FRAME,
+ BQ_CORNER, BK_ROW, BK_FRAME, BK_CORNER, A2A_B, SUM_QUAD, SUM_Z, SPREAD) = range(24)
 FAR_FIRST = (8, 7, 9, 6, 10, 5, 11, 4, 12, 3, 13, 2, 14, 1, 15)
 KV_SPANS = ((0, 32), (32, 32), (64, 32))
 Q_SPANS = ((96, 64), (160, 64), (224, 32))
@@ -68,7 +68,7 @@
 
 
 def kernel(x_ref, g_ref, w_ref, gain_ref, gx_ref, gw_ref, gg_ref,
-           xv, wf, wt, sb, rb, xs, xr, xf, pe, hs, hr, norm, kvg, qgr, raised_ref, ga_ref, st, dqb, dqr, zb, zr,
+           xv, wf, wt, sbk, rbk, sbq, rbq, xs, xr, xf, pe, hs, hr, norm, kvg, qgr, raised_ref, ga_ref, st, dqb, dqr, zb, zr,
            hb, hbr, ge, exh, sb2, rb2, gall, ex, gxv, wg, wb, kr, zs, fr, flat, gsc, ss, rs, local):
     s = lax.axis_index("seq")
     n = lax.axis_index("head")
@@ -137,6 +137,27 @@
     def fine(m, f, r):
         return xv[(f * 4 + r) * 3 + m].astype(F32)
 
+    def store_heads(dst, groups):
+        for p in range(len(groups) // 2):
+            v = jnp.concatenate(groups[2 * p:2 * p + 2], 0)
+            for h, part in enumerate(split_heads(tiles_of(v))):
+                dst[h, p * 16:p * 16 + 16, :] = part.astype(BF16)
+
+    groups = []
+    for t in range(2):
+        for y in range(2):
+            both = []
+            for m in (1, 2):
+                k_sum = None
+                for f, a in PAIRS_K[t]:
+                    for r, b in PAIRS_K[y]:
+                        tk = fine(m, f, r) * wt[1 + m, a * 3 + b]
+                        k_sum = tk if k_sum is None else k_sum + tk
+                t1 = k_sum + up(k_sum, 1)
+                both.append(jnp.where(row == 0, t1, jnp.where(row == 1, up(t1, 2) + up(k_sum, 4), jnp.where(
+                    row == 2, up(k_sum, 5), 0.0))))
+            groups.append(both[0] + pltpu.roll(both[1], 4, 0))
+    store_heads(sbk, groups)
     groups = []
     for t in range(3):
         for y in range(3):
@@ -152,33 +173,10 @@
             v = jnp.where(row == 0, e, jnp.where(row == 1, up(e, 1), jnp.where(row == 2, up(e, 2), jnp.where(
                 row == 3, up(e, 3), jnp.where(row == 4, up(b1, 4), 0.0)))))
             groups.append(v)
-    for t in range(2):
-        for y in range(2):
-            both = []
-            for m in (1, 2):
-                k_sum = None
-                for f, a in PAIRS_K[t]:
-                    for r, b in PAIRS_K[y]:
-                        tk = fine(m, f, r) * wt[1 + m, a * 3 + b]
-                        k_sum = tk if k_sum is None else k_sum + tk
-                t1 = k_sum + up(k_sum, 1)
-                both.append(jnp.where(row == 0, t1, jnp.where(row == 1, up(t1, 2) + up(k_sum, 4), jnp.where(
-                    row == 2, up(k_sum, 5), 0.0))))
-            groups.append(both[0] + pltpu.roll(both[1], 4, 0))
     groups.append(jnp.zeros((8, 768), F32))
     for t in range(2):
         groups.append(jnp.concatenate([g_ref[t, 0].astype(F32), g_ref[t, 1].astype(F32)], 0))
-    for p in range(8):
-        v = jnp.concatenate(groups[2 * p:2 * p + 2], 0)
-        for h, part in enumerate(split_heads(tiles_of(v))):
-            sb[h, p * 16:p * 16 + 16, :] = part.astype(BF16)
-
-    pl.semaphore_wait(barrier, len(greeted))
-    for k in range(1, HEADS):
-        peer = head_peer(k)
-        send(A2A_F, sb.at[peer[1]], rb.at[k], peer)
-    pending.append((A2A_F, rb.at[pl.ds(1, HEADS - 1)]))
-    rb[0] = sb[n]
+    store_heads(sbq, groups)
 
     def split_fine(p, carry):
         v = jnp.concatenate([xv[2 * p].astype(F32), xv[2 * p + 1].astype(F32)], 0)
@@ -186,12 +184,20 @@
             xs[h, pl.ds(pl.multiple_of(p * 16, 16), 16), :] = part.astype(BF16)
         return carry
     lax.fori_loop(0, 24, split_fine, 0)
-    arrived(A2A_F, rb.at[pl.ds(1, HEADS - 1)])
+
+    pl.semaphore_wait(barrier, len(greeted))
+    for stage, src, dst in ((A2A_K, sbk, rbk), (A2A_Q, sbq, rbq)):
+        for k in (4, 5, 3, 7, 1, 2, 6):
+            peer = head_peer(k)
+            send(stage, src.at[peer[1]], dst.at[k], peer)
+        pending.append((stage, dst.at[pl.ds(1, HEADS - 1)]))
+        dst[0] = src[n]
+    arrived(A2A_K, rbk.at[pl.ds(1, HEADS - 1)])
 
     from_col = [lax.rem(n - h + HEADS, HEADS) for h in range(HEADS)]
-    sets = [rb[from_col[h]].astype(F32) for h in range(HEADS)]
+    sets = [rbk[from_col[h]].astype(F32) for h in range(HEADS)]
     for grp in range(4):
-        parts = [v[72 + grp * 8:80 + grp * 8] for v in sets]
+        parts = [v[grp * 8:grp * 8 + 8] for v in sets]
         for m in range(2):
             if m == 0:
                 own = [jnp.where(row8 < 4, p, 0.0) for p in parts]
@@ -224,6 +230,8 @@
 
     hs[0:96, :] = jnp.concatenate([pkv(0, 1), pkv(1, 0), pkv(1, 1)], 0).astype(BF16)
     exchange((KV_ROW, KV_FRAME, KV_CORNER), KV_SPANS, hs, hr, (1, 16, 17))
+    arrived(A2A_Q, rbq.at[pl.ds(1, HEADS - 1)])
+    sets = [rbq[from_col[h]].astype(F32) for h in range(HEADS)]
     for grp in range(9):
         parts = [v[grp * 8:grp * 8 + 8] for v in sets]
         rolled = [pltpu.roll(parts[2 * j + 1], 4, 0) for j in range(4)]
@@ -244,7 +252,7 @@
         for y in range(2):
             vs = []
             for j in range(4):
-                a, b = (sets[2 * j + i][112 + t * 8:120 + t * 8] for i in range(2))
+                a, b = (sets[2 * j + i][80 + t * 8:88 + t * 8] for i in range(2))
                 if y == 0:
                     vs.append(jnp.where(row8 < 4, a, pltpu.roll(b, 4, 0)))
                 else:
@@ -407,20 +415,26 @@
             tap_rows((jnp.where(row64 % 2 == 1, second, 0.0), jnp.where(row64 % 2 == 0, first, 0.0),
                       jnp.where(row64 % 2 == 1, first, 0.0)), 0, a * 3 + b)
 
+    def key_taps(m, wide, chosen):
+        for a, b in chosen:
+            (f, t), = pairs(PAIRS_K, a)
+            (rr, y), = pairs(PAIRS_K, b)
+            v = xf[(f * 4 + rr) * 3 + m] * wide[t * 2 + y]
+            tap_rows(tuple(jnp.where(row64 % 4 == c, v, 0.0) for c in (3, 0, 1)), m, a * 3 + b)
+
+    def wide_key(m, group):
+        at = 224 + m * 64 + group * 16
+        return jnp.dot(spread_k, ge[at:at + 16, :].astype(BF16), preferred_element_type=F32)
+
+    for m in (1, 2):
+        key_taps(m, (wide_key(m, 0),), ((1, 1), (1, 2), (2, 1), (2, 2)))
     exchanged((BK_ROW, BK_FRAME, BK_CORNER), KV_SPANS, hbr)
     for lo, at, has in ((0, 16, back_u), (32, 32, back_g), (64, 48, back_c)):
         v = returned(lo, 32, has)
         ge[288 + at:304 + at, :] = v[0:16]
         ge[352 + at:368 + at, :] = v[16:32]
     for m in (1, 2):
-        wide = [jnp.dot(spread_k, ge[at:at + 16, :].astype(BF16), preferred_element_type=F32)
-                for at in range(224 + m * 64, 288 + m * 64, 16)]
-        for a in range(3):
-            for b in range(3):
-                (f, t), = pairs(PAIRS_K, a)
-                (rr, y), = pairs(PAIRS_K, b)
-                v = xf[(f * 4 + rr) * 3 + m] * wide[t * 2 + y]
-                tap_rows(tuple(jnp.where(row64 % 4 == c, v, 0.0) for c in (3, 0, 1)), m, a * 3 + b)
+        key_taps(m, (None,) + tuple(wide_key(m, group) for group in (1, 2, 3)), ((0, 0), (0, 1), (0, 2), (1, 0), (2, 0)))
 
     t16, t8 = wg[64:80, :], wg[80:88, :]
     tail = jnp.concatenate([pltpu.roll(t16, 96, 1), pltpu.roll(t16, 64, 1), pltpu.roll(t16, 32, 1),
@@ -506,7 +520,7 @@
     v = zs[z].astype(F32)
     for k in range(1, ZS):
         v = v + zs[lax.rem(z - k + ZS, ZS)].astype(F32)
-    fr[0] = v
+    fr[0] = v.astype(BF16)
     for p in range(31, 0, -1):
         send(SPREAD, fr.at[0], fr.at[p], plane_peer(p))
     pending.append((SPREAD, fr.at[pl.ds(1, 31)]))
@@ -515,7 +529,7 @@
     lane16 = iota((16, 128), 1)
     unpacked, gains = [], None
     for h in range(HEADS):
-        at = [fr[lax.rem(yl + q // 2, 2) * (2 * HEADS) + lax.rem(core + q % 2, 2) * HEADS + from_col[h]] for q in range(4)]
+        at = [fr[lax.rem(yl + q // 2, 2) * (2 * HEADS) + lax.rem(core + q % 2, 2) * HEADS + from_col[h]].astype(F32) for q in range(4)]
         t16 = jnp.where(lane16 < 32, pltpu.roll(at[0], 32, 1), jnp.where(
             lane16 < 64, pltpu.roll(at[1], 64, 1), pltpu.roll(at[2], 96, 1)))
         lo, hi = at[3][0:8], at[3][8:16]
@@ -542,8 +556,10 @@
         ((48, 8, 768), BF16),
         ((3, 27, 768), F32),
         ((4, 9, 8, 768), F32),
-        ((8, 128, 128), BF16),
-        ((8, 128, 128), BF16),
+        ((8, 32, 128), BF16),
+        ((8, 32, 128), BF16),
+        ((8, 96, 128), BF16),
+        ((8, 96, 128), BF16),
         ((8, 384, 128), BF16),
         ((8, 384, 128), BF16),
         ((48, 64, 128), F32),
@@ -573,7 +589,7 @@
         ((64, 128), F32),
         ((4, 16, 128), F32),
         ((ZS, 16, 128), BF16),
-        ((32, 16, 128), F32),
+        ((32, 16, 128), BF16),
         ((6 * 88, 128), F32),
         ((8, 128), F32),
     ]
@@ -584,7 +600,7 @@
         in_specs=[hbm] + [vmem] * 3,
         out_specs=(hbm, vmem, vmem),
         scratch_shapes=[pltpu.VMEM(shape, kind) for shape, kind in scratch]
-        + [pltpu.SemaphoreType.DMA((23,)), pltpu.SemaphoreType.DMA((23,)), pltpu.SemaphoreType.DMA((2,))],
+        + [pltpu.SemaphoreType.DMA((24,)), pltpu.SemaphoreType.DMA((24,)), pltpu.SemaphoreType.DMA((2,))],
         compiler_params=pltpu.CompilerParams(collective_id=0, has_side_effects=True,
                                              vmem_limit_bytes=60 * 1024 * 1024),
     )(x, grad_out[0], w, norm_gain)

time: 82.9 us -> 81.2 us (0.979)
  Pallas kernels: 78.7 us -> 77.1 us
    pallas_call x1, Pallas kernels: 78.7 us -> 77.1 us  [shards(): pl.pallas_call(kernel, out_shape=(jax.ShapeDtypeStruct(x.shape, BF16), ja...]
where the time goes in v3:
time: 81.2 us; the launch traced here: 81 us
  Pallas kernels  77.1 us (95%)
  local copies, waits for them, and re-layouts  3.26 us (4%)
    pallas_call x1, Pallas kernels, shards(): pl.pallas_call(kernel, out_shape=(jax.ShapeDtypeStruct(x.shape, BF16), ja...  77.1 us
    unnamed x7, local copies, waits for them, and re-layouts  3.26 us

profile of v3, /device:TPU:1, one launch (start us, length us, event | category | flops | bytes accessed | tf_op | source)
XLA Modules:
  0.0 81.0 jit_solution(12366092506370721408)
XLA Ops:
  0.6 77.1 %shard_map.67 = (bf16[48,8,768]{2,1,0:T(8,128)(2,1)}, f32[3,27,768]{2,1,0:T(8,128)}, f32[3,96]{1,0:T(4,128)}) custom-call(bf16[48,8,768]{2,1,0:T(8,128)(2,1)} %bitcast.13, bf16[2,2,4,768]{3,2,1,0:T(4,128)(2,1)} %bitcast.17, bf16[3,27,768]{2,1,0:T(8,128)(2,1)} %bitcast.16, f32[3,96]{1,0:T(4,128)} %gain_ref.1), custom_call_target="tpu_custom_call" | custom-call | tf_op jit(solution)/shard_map/pallas_call | solution.py:596
  77.7 0.0 copy-start
  77.7 2.0 %copy.10 = bf16[1,4,4,8,3,768]{5,3,4,2,1,0:T(8,128)(2,1)} copy(bf16[1,4,4,8,3,768]{5,3,4,2,1,0:T(8,128)(2,1)} %bitcast.14) | data formatting | bytes 1179648
  79.7 0.0 copy-done
  79.7 0.0 copy-start.1
  79.7 0.7 copy.11
  80.4 0.0 copy-done.1
  80.4 0.6 copy.12
Async XLA Ops:
  77.7 2.0 %copy-start = (f32[3,27,768]{2,1,0:T(8,128)S(1)}, f32[3,27,768]{2,1,0:T(8,128)}, u32[]{:S(2)}) copy-start(f32[3,27,768]{2,1,0:T(8,128)} %get-tuple-element.7) | copy-start | bytes 746500
  79.7 0.7 copy-start.1

commit v4 on v3

--- a/solution.py
+++ b/solution.py
@@ -19,11 +19,12 @@
 PAIRS_K = (((0, 1), (1, 2)), ((3, 0),))
 OWN_Q = (0, 1, 3, 4)
 
-(A2A_K, A2A_Q, FINE, KV_ROW, KV_FRAME, KV_CORNER, Q_ROW, Q_FRAME, Q_CORNER, GATHER, QUAD, STATS, DQ, SCATTER, BQ_ROW, BQ_FRAME,
- BQ_CORNER, BK_ROW, BK_FRAME, BK_CORNER, A2A_B, SUM_QUAD, SUM_Z, SPREAD) = range(24)
+(A2A_K, A2A_Q, FINE, KV_OWN, KV_ROW, KV_FRAME, KV_CORNER, Q_ROW, Q_FRAME, Q_CORNER, GATHER, QUAD, STATS, DQ, SCATTER,
+ BQ_ROW, BQ_FRAME, BQ_CORNER, BK_OWN, BK_ROW, BK_FRAME, BK_CORNER, A2A_B, SUM_QUAD, SUM_Z, SPREAD) = range(26)
 FAR_FIRST = (8, 7, 9, 6, 10, 5, 11, 4, 12, 3, 13, 2, 14, 1, 15)
-KV_SPANS = ((0, 32), (32, 32), (64, 32))
-Q_SPANS = ((96, 64), (160, 64), (224, 32))
+KV_SPANS = ((0, 32), (32, 32), (64, 32), (96, 32))
+Q_SPANS = ((128, 64), (192, 64), (256, 32))
+HALF_WAY = 12
 
 
 def iota(shape, dim):
@@ -96,8 +97,19 @@
     def seq_peer(d):
         return (lax.rem(s + d + SEQ, SEQ), n)
 
+    def owner(d):
+        block = lax.rem(s + d, SEQ)
+        return (block // (2 * ZS) * (2 * ZS) + lax.rem(block // 2 % ZS + HALF_WAY, ZS) * 2 + block % 2, n)
+
+    owned = yl * (2 * ZS) + lax.rem(z + ZS - HALF_WAY, ZS) * 2 + core
+
+    def feeder(d):
+        return (lax.rem(owned - d + SEQ, SEQ), n)
+
+
     barrier = pltpu.get_barrier_semaphore()
     greeted = [seq_peer(d) for d in (16, 17, -16, -17)] + [z_peer(k) for k in FAR_FIRST]
+    greeted += [owner(d) for d in (17, 16, 1)] + [feeder(d) for d in (17, 16, 1)]
     greeted += [seq_peer(1), seq_peer(-1)] + [quad_peer(k) for k in (3, 2, 1)] + [head_peer(k) for k in range(1, HEADS)]
     for peer in greeted:
         pl.semaphore_signal(barrier, inc=1, device_id=peer, device_id_type=MESH)
@@ -219,17 +231,17 @@
         at = 288 + (t * 2 + y) * 16
         return jnp.concatenate([pe[at:at + 16, :], pe[at + 64:at + 80, :]], 0)
 
-    def exchange(stages, spans, src, dst, distances):
-        for stage, (lo, count), d in zip(stages, spans, distances):
-            send(stage, src.at[pl.ds(lo, count)], dst.at[pl.ds(lo, count)], seq_peer(d))
+    def exchange(stages, spans, src, dst, peers):
+        for stage, (lo, count), peer in zip(stages, spans, peers):
+            send(stage, src.at[pl.ds(lo, count)], dst.at[pl.ds(lo, count)], peer)
             pending.append((stage, dst.at[pl.ds(lo, count)]))
 
     def exchanged(stages, spans, dst):
         for stage, (lo, count) in zip(stages, spans):
             arrived(stage, dst.at[pl.ds(lo, count)])
 
-    hs[0:96, :] = jnp.concatenate([pkv(0, 1), pkv(1, 0), pkv(1, 1)], 0).astype(BF16)
-    exchange((KV_ROW, KV_FRAME, KV_CORNER), KV_SPANS, hs, hr, (1, 16, 17))
+    hs[0:128, :] = jnp.concatenate([pkv(0, 0), pkv(0, 1), pkv(1, 0), pkv(1, 1)], 0).astype(BF16)
+    exchange((KV_OWN, KV_ROW, KV_FRAME, KV_CORNER), KV_SPANS, hs, hr, [owner(d) for d in (0, 1, 16, 17)])
     arrived(A2A_Q, rbq.at[pl.ds(1, HEADS - 1)])
     sets = [rbq[from_col[h]].astype(F32) for h in range(HEADS)]
     for grp in range(9):
@@ -240,8 +252,8 @@
             if j:
                 v = v + jnp.where(row8 == 0, rolled[j - 1], 0.0)
             pe[grp * 32 + j * 8:grp * 32 + j * 8 + 8, :] = v
-    hs[96:256, :] = jnp.concatenate([pq(0, 2), pq(1, 2), pq(2, 0), pq(2, 1), pq(2, 2)], 0).astype(BF16)
-    exchange((Q_ROW, Q_FRAME, Q_CORNER), Q_SPANS, hs, hr, (1, 16, 17))
+    hs[128:288, :] = jnp.concatenate([pq(0, 2), pq(1, 2), pq(2, 0), pq(2, 1), pq(2, 2)], 0).astype(BF16)
+    exchange((Q_ROW, Q_FRAME, Q_CORNER), Q_SPANS, hs, hr, [seq_peer(d) for d in (1, 16, 17)])
     for k in range(1, HEADS):
         peer = head_peer(k)
         send(FINE, xs.at[peer[1]], xr.at[k], peer)
@@ -276,18 +288,21 @@
     def border(lo, count, has):
         return hr[lo:lo + count, :].astype(F32) * has
 
-    exchanged((KV_ROW, KV_FRAME, KV_CORNER), KV_SPANS, hr)
+    exchanged((KV_OWN, KV_ROW, KV_FRAME, KV_CORNER), KV_SPANS, hr)
+    own_u = (owned % ROW_GROUPS > 0).astype(F32)
+    own_g = (owned // ROW_GROUPS > 0).astype(F32)
     gain_kv = jnp.where(iota((32, 128), 0) < 16, gsc[1:2, :], gsc[2:3, :])
     gain_q = jnp.broadcast_to(gsc[0:1, :], (128, 128))
-    kvg[0] = layer_norm(pkv(0, 0) + border(0, 32, has_u) + border(32, 32, has_g) + border(64, 32, has_c), 128, 32, gain_kv)
+    kvg[0] = layer_norm(hr[0:32, :].astype(F32) + border(32, 32, own_u) + border(64, 32, own_g) + border(96, 32, own_u * own_g),
+                        128, 32, gain_kv)
     for k in FAR_FIRST:
         send(GATHER, kvg.at[0], kvg.at[k], z_peer(k))
     pending.append((GATHER, kvg.at[pl.ds(1, ZS - 1)]))
 
     exchanged((Q_ROW, Q_FRAME, Q_CORNER), Q_SPANS, hr)
-    q00 = pq(0, 0) + border(96, 32, has_u) + border(160, 32, has_g) + border(224, 32, has_c)
-    q01 = pq(0, 1) + border(192, 32, has_g)
-    q10 = pq(1, 0) + border(128, 32, has_u)
+    q00 = pq(0, 0) + border(128, 32, has_u) + border(192, 32, has_g) + border(256, 32, has_c)
+    q01 = pq(0, 1) + border(224, 32, has_g)
+    q10 = pq(1, 0) + border(160, 32, has_u)
     qgr[0, 0:128, :] = layer_norm(jnp.concatenate([q00, q01, q10, pq(1, 1)], 0), 0, 128, gain_q)
     for k in (2, 3, 1):
         send(QUAD, qgr.at[0], qgr.at[k], quad_peer(k))
@@ -355,8 +370,8 @@
     gq, gain_rows = norm_backward(dq * SCALE + qgr[0, 128:256, :].astype(F32), 0, 128, gain_q)
     wg[80:88, :] = jnp.zeros((8, 128), F32)
     wg[81:82, :] = jnp.sum(gain_rows, 0, keepdims=True)
-    hb[96:256, :] = jnp.concatenate([gq[0:32], gq[64:96], gq[0:64], gq[0:32]], 0).astype(BF16)
-    exchange((BQ_ROW, BQ_FRAME, BQ_CORNER), Q_SPANS, hb, hbr, (-1, -16, -17))
+    hb[128:288, :] = jnp.concatenate([gq[0:32], gq[64:96], gq[0:64], gq[0:32]], 0).astype(BF16)
+    exchange((BQ_ROW, BQ_FRAME, BQ_CORNER), Q_SPANS, hb, hbr, [seq_peer(-d) for d in (1, 16, 17)])
     for i, grp in enumerate(OWN_Q):
         ge[grp * 32:grp * 32 + 32, :] = gq[i * 32:i * 32 + 32]
 
@@ -368,10 +383,8 @@
     gkv, gain_rows = norm_backward(jnp.sum(zr[...].astype(F32), 0), 128, 32, gain_kv)
     wg[82:83, :] = jnp.sum(gain_rows[0:16], 0, keepdims=True)
     wg[83:84, :] = jnp.sum(gain_rows[16:32], 0, keepdims=True)
-    hb[0:96, :] = jnp.concatenate([gkv, gkv, gkv], 0).astype(BF16)
-    exchange((BK_ROW, BK_FRAME, BK_CORNER), KV_SPANS, hb, hbr, (-1, -16, -17))
-    ge[288:304, :] = gkv[0:16]
-    ge[352:368, :] = gkv[16:32]
+    hb[0:128, :] = jnp.concatenate([gkv] * 4, 0).astype(BF16)
+    exchange((BK_OWN, BK_ROW, BK_FRAME, BK_CORNER), KV_SPANS, hb, hbr, [feeder(d) for d in (0, 1, 16, 17)])
     back_u = (u < ROW_GROUPS - 1).astype(F32)
     back_g = (group < SEQ // ROW_GROUPS - 1).astype(F32)
     back_c = back_u * back_g
@@ -380,10 +393,10 @@
         return hbr[lo:lo + count, :].astype(F32) * has
 
     exchanged((BQ_ROW, BQ_FRAME, BQ_CORNER), Q_SPANS, hbr)
-    ge[2 * 32:3 * 32, :] = returned(96, 32, back_u)
-    ge[5 * 32:6 * 32, :] = returned(128, 32, back_u)
-    ge[6 * 32:8 * 32, :] = returned(160, 64, back_g)
-    ge[8 * 32:9 * 32, :] = returned(224, 32, back_c)
+    ge[2 * 32:3 * 32, :] = returned(128, 32, back_u)
+    ge[5 * 32:6 * 32, :] = returned(160, 32, back_u)
+    ge[6 * 32:8 * 32, :] = returned(192, 64, back_g)
+    ge[8 * 32:9 * 32, :] = returned(256, 32, back_c)
 
     def pairs(pair_list, a):
         return [(f, t) for t, entries in enumerate(pair_list) for f, tap in entries if tap == a]
@@ -426,15 +439,13 @@
         at = 224 + m * 64 + group * 16
         return jnp.dot(spread_k, ge[at:at + 16, :].astype(BF16), preferred_element_type=F32)
 
-    for m in (1, 2):
-        key_taps(m, (wide_key(m, 0),), ((1, 1), (1, 2), (2, 1), (2, 2)))
-    exchanged((BK_ROW, BK_FRAME, BK_CORNER), KV_SPANS, hbr)
-    for lo, at, has in ((0, 16, back_u), (32, 32, back_g), (64, 48, back_c)):
+    exchanged((BK_OWN, BK_ROW, BK_FRAME, BK_CORNER), KV_SPANS, hbr)
+    for lo, at, has in ((0, 0, 1.0), (32, 16, back_u), (64, 32, back_g), (96, 48, back_c)):
         v = returned(lo, 32, has)
         ge[288 + at:304 + at, :] = v[0:16]
         ge[352 + at:368 + at, :] = v[16:32]
     for m in (1, 2):
-        key_taps(m, (None,) + tuple(wide_key(m, group) for group in (1, 2, 3)), ((0, 0), (0, 1), (0, 2), (1, 0), (2, 0)))
+        key_taps(m, [wide_key(m, group) for group in range(4)], [(a, b) for a in range(3) for b in range(3)])
 
     t16, t8 = wg[64:80, :], wg[80:88, :]
     tail = jnp.concatenate([pltpu.roll(t16, 96, 1), pltpu.roll(t16, 64, 1), pltpu.roll(t16, 32, 1),
@@ -564,8 +575,8 @@
         ((8, 384, 128), BF16),
         ((48, 64, 128), F32),
         ((416, 128), F32),
-        ((256, 128), BF16),
-        ((256, 128), BF16),
+        ((288, 128), BF16),
+        ((288, 128), BF16),
         ((2, 160, 128), F32),
         ((ZS, 32, 128), BF16),
         ((4, 256, 128), BF16),
@@ -576,8 +587,8 @@
         ((4, 128, 128), F32),
         ((ZS, 32, 128), BF16),
         ((ZS, 32, 128), BF16),
-        ((256, 128), BF16),
-        ((256, 128), BF16),
+        ((288, 128), BF16),
+        ((288, 128), BF16),
         ((416, 128), F32),
         ((9 * 128, 128), F32),
         ((8, 112, 128), BF16),
@@ -600,7 +611,7 @@
         in_specs=[hbm] + [vmem] * 3,
         out_specs=(hbm, vmem, vmem),
         scratch_shapes=[pltpu.VMEM(shape, kind) for shape, kind in scratch]
-        + [pltpu.SemaphoreType.DMA((24,)), pltpu.SemaphoreType.DMA((24,)), pltpu.SemaphoreType.DMA((2,))],
+        + [pltpu.SemaphoreType.DMA((26,)), pltpu.SemaphoreType.DMA((26,)), pltpu.SemaphoreType.DMA((2,))],
         compiler_params=pltpu.CompilerParams(collective_id=0, has_side_effects=True,
                                              vmem_limit_bytes=60 * 1024 * 1024),
     )(x, grad_out[0], w, norm_gain)

time: 81.2 us -> 77.4 us (0.953)
  Pallas kernels: 77.1 us -> 73.3 us
    pallas_call x1, Pallas kernels: 77.1 us -> 73.3 us  [shards(): pl.pallas_call(kernel, out_shape=(jax.ShapeDtypeStruct(x.shape, BF16), ja...]
where the time goes in v4:
time: 77.4 us; the launch traced here: 77.2 us
  Pallas kernels  73.3 us (95%)
  local copies, waits for them, and re-layouts  3.26 us (4%)
    pallas_call x1, Pallas kernels, shards(): pl.pallas_call(kernel, out_shape=(jax.ShapeDtypeStruct(x.shape, BF16), ja...  73.3 us
    unnamed x7, local copies, waits for them, and re-layouts  3.26 us

profile of v4, /device:TPU:1, one launch (start us, length us, event | category | flops | bytes accessed | tf_op | source)
XLA Modules:
  0.0 77.2 jit_solution(5526742304621046530)
XLA Ops:
  0.6 73.3 %shard_map.67 = (bf16[48,8,768]{2,1,0:T(8,128)(2,1)}, f32[3,27,768]{2,1,0:T(8,128)}, f32[3,96]{1,0:T(4,128)}) custom-call(bf16[48,8,768]{2,1,0:T(8,128)(2,1)} %bitcast.13, bf16[2,2,4,768]{3,2,1,0:T(4,128)(2,1)} %bitcast.17, bf16[3,27,768]{2,1,0:T(8,128)(2,1)} %bitcast.16, f32[3,96]{1,0:T(4,128)} %gain_ref.1), custom_call_target="tpu_custom_call" | custom-call | tf_op jit(solution)/shard_map/pallas_call | solution.py:607
  73.9 0.0 copy-start
  74.0 2.0 %copy.10 = bf16[1,4,4,8,3,768]{5,3,4,2,1,0:T(8,128)(2,1)} copy(bf16[1,4,4,8,3,768]{5,3,4,2,1,0:T(8,128)(2,1)} %bitcast.14) | data formatting | bytes 1179648
  75.9 0.0 copy-done
  75.9 0.0 copy-start.1
  75.9 0.7 copy.11
  76.6 0.0 copy-done.1
  76.6 0.6 copy.12
Async XLA Ops:
  73.9 2.0 %copy-start = (f32[3,27,768]{2,1,0:T(8,128)S(1)}, f32[3,27,768]{2,1,0:T(8,128)}, u32[]{:S(2)}) copy-start(f32[3,27,768]{2,1,0:T(8,128)} %get-tuple-element.7) | copy-start | bytes 746500
  75.9 0.7 copy-start.1

commit v5 on v4

--- a/solution.py
+++ b/solution.py
@@ -68,16 +68,18 @@
     return [v[:, j * 128:(j + 1) * 128] for j in range(6)]
 
 
-def kernel(x_ref, g_ref, w_ref, gain_ref, gx_ref, gw_ref, gg_ref,
-           xv, wf, wt, sbk, rbk, sbq, rbq, xs, xr, xf, pe, hs, hr, norm, kvg, qgr, raised_ref, ga_ref, st, dqb, dqr, zb, zr,
-           hb, hbr, ge, exh, sb2, rb2, gall, ex, gxv, wg, wb, kr, zs, fr, flat, gsc, ss, rs, local):
+def kernel(x_ref, g_hbm, w_hbm, gain_hbm, gx_ref, gw_ref, gg_ref,
+           xv, g_ref, w_ref, gain_ref, wf, wt, sbk, rbk, sbq, rbq, xs, xr, xf, pe, hs, hr, norm, kvg, qgr, raised_ref, ga_ref, st, dqb, dqr, zb, zr,
+           hb, hbr, ge, exh, sb2, rb2, gall, ex, gxv, wg, wb, kr, zs, fr, flat, gsc, ss, rs, local, ready):
     s = lax.axis_index("seq")
     n = lax.axis_index("head")
     group, u = s // ROW_GROUPS, s % ROW_GROUPS
     yl, z, core = s // (2 * ZS), s // 2 % ZS, s % 2
 
-    load = pltpu.make_async_copy(x_ref, xv, local.at[0])
-    load.start()
+    loads = [pltpu.make_async_copy(src, dst, local.at[i]) for i, (src, dst) in enumerate(
+        ((w_hbm, w_ref), (gain_hbm, gain_ref), (x_ref, xv), (g_hbm, g_ref)))]
+    for load in loads:
+        load.start()
 
     def head_peer(k):
         return (s, lax.rem(n + k, HEADS))
@@ -108,7 +110,7 @@
 
 
     barrier = pltpu.get_barrier_semaphore()
-    greeted = [seq_peer(d) for d in (16, 17, -16, -17)] + [z_peer(k) for k in FAR_FIRST]
+    greeted = [z_peer(k) for k in (4, 12, 3, 13, 2, 14, 1, 15)]
     greeted += [owner(d) for d in (17, 16, 1)] + [feeder(d) for d in (17, 16, 1)]
     greeted += [seq_peer(1), seq_peer(-1)] + [quad_peer(k) for k in (3, 2, 1)] + [head_peer(k) for k in range(1, HEADS)]
     for peer in greeted:
@@ -121,6 +123,11 @@
     def arrived(stage, ref):
         pltpu.make_async_copy(ref, ref, rs.at[stage]).wait()
 
+    def hand_on(stage, peers):
+        for peer in peers:
+            pl.semaphore_signal(ready.at[stage], inc=1, device_id=peer, device_id_type=MESH)
+
+    quad, four_on = [quad_peer(k) for k in (2, 3, 1)], [z_peer(4), z_peer(12)]
     pending = []
 
     def drain():
@@ -130,6 +137,7 @@
     row = iota((8, 768), 0)
     row8 = iota((8, 128), 0)
     lane8 = iota((8, 128), 1)
+    loads[0].wait()
     wf[...] = w_ref[...].astype(F32)
 
     def taps(ab, carry):
@@ -142,9 +150,11 @@
                 row % 4 == 1, one(m, 2), jnp.where(row % 4 == 3, one(m, 0), 0.0)))
         return carry
     lax.fori_loop(0, 9, taps, 0)
+    loads[1].wait()
     gsc[...] = jnp.zeros_like(gsc)
     gsc[0:3, 0:HD] = gain_ref[...]
-    load.wait()
+    loads[2].wait()
+    loads[3].wait()
 
     def fine(m, f, r):
         return xv[(f * 4 + r) * 3 + m].astype(F32)
@@ -204,6 +214,9 @@
             send(stage, src.at[peer[1]], dst.at[k], peer)
         pending.append((stage, dst.at[pl.ds(1, HEADS - 1)]))
         dst[0] = src[n]
+    hand_on(0, quad)
+    pl.semaphore_wait(ready.at[0], 3)
+    hand_on(1, four_on)
     arrived(A2A_K, rbk.at[pl.ds(1, HEADS - 1)])
 
     from_col = [lax.rem(n - h + HEADS, HEADS) for h in range(HEADS)]
@@ -242,6 +255,8 @@
 
     hs[0:128, :] = jnp.concatenate([pkv(0, 0), pkv(0, 1), pkv(1, 0), pkv(1, 1)], 0).astype(BF16)
     exchange((KV_OWN, KV_ROW, KV_FRAME, KV_CORNER), KV_SPANS, hs, hr, [owner(d) for d in (0, 1, 16, 17)])
+    pl.semaphore_wait(ready.at[1], 2)
+    hand_on(2, four_on)
     arrived(A2A_Q, rbq.at[pl.ds(1, HEADS - 1)])
     sets = [rbq[from_col[h]].astype(F32) for h in range(HEADS)]
     for grp in range(9):
@@ -253,6 +268,7 @@
                 v = v + jnp.where(row8 == 0, rolled[j - 1], 0.0)
             pe[grp * 32 + j * 8:grp * 32 + j * 8 + 8, :] = v
     hs[128:288, :] = jnp.concatenate([pq(0, 2), pq(1, 2), pq(2, 0), pq(2, 1), pq(2, 2)], 0).astype(BF16)
+    pl.semaphore_wait(ready.at[2], 2)
     exchange((Q_ROW, Q_FRAME, Q_CORNER), Q_SPANS, hs, hr, [seq_peer(d) for d in (1, 16, 17)])
     for k in range(1, HEADS):
         peer = head_peer(k)
@@ -407,7 +423,11 @@
     r = iota((128, 32), 0)
     spread_q = spread(128, 32, ((r & 63) >> 1) + (r >> 6))
     spread_k = spread(64, 16, (iota((64, 16), 0) + 1) >> 2)
-    row64 = iota((64, 128), 0)
+    odd, by_four = row8 % 2 == 1, row8 % 4
+
+    def over_blocks(v):
+        return jnp.sum(v.reshape(HEADS, 8, 128), 0)
+
     for grp in range(9):
         exh[grp * 128:grp * 128 + 128, :] = jnp.dot(spread_q, ge[grp * 32:grp * 32 + 32, :].astype(BF16),
                                                     preferred_element_type=F32)
@@ -425,15 +445,15 @@
                     t1, t2 = v * exh[at:at + 64, :], v * exh[at + 64:at + 128, :]
                     first = t1 if first is None else first + t1
                     second = t2 if second is None else second + t2
-            tap_rows((jnp.where(row64 % 2 == 1, second, 0.0), jnp.where(row64 % 2 == 0, first, 0.0),
-                      jnp.where(row64 % 2 == 1, first, 0.0)), 0, a * 3 + b)
+            first, second = over_blocks(first), over_blocks(second)
+            tap_rows((jnp.where(odd, second, 0.0), jnp.where(odd, 0.0, first), jnp.where(odd, first, 0.0)), 0, a * 3 + b)
 
     def key_taps(m, wide, chosen):
         for a, b in chosen:
             (f, t), = pairs(PAIRS_K, a)
             (rr, y), = pairs(PAIRS_K, b)
-            v = xf[(f * 4 + rr) * 3 + m] * wide[t * 2 + y]
-            tap_rows(tuple(jnp.where(row64 % 4 == c, v, 0.0) for c in (3, 0, 1)), m, a * 3 + b)
+            v = over_blocks(xf[(f * 4 + rr) * 3 + m] * wide[t * 2 + y])
+            tap_rows(tuple(jnp.where(by_four == c, v, 0.0) for c in (3, 0, 1)), m, a * 3 + b)
 
     def wide_key(m, group):
         at = 224 + m * 64 + group * 16
@@ -524,7 +544,7 @@
                     for y, b in reached(PAIRS_K, rr):
                         k_sum = g_at(9 + t * 2 + y, m - 1) * wt[1 + m, a * 3 + b]
                 gxv[(f * 4 + rr) * 3 + m] = k_sum.astype(BF16)
-    store = pltpu.make_async_copy(gxv, gx_ref, local.at[1])
+    store = pltpu.make_async_copy(gxv, gx_ref, local.at[4])
     store.start()
 
     arrived(SUM_Z, zs.at[pl.ds(1, ZS - 1)])
@@ -565,6 +585,9 @@
     hbm = pl.BlockSpec(memory_space=pl.ANY)
     scratch = [
         ((48, 8, 768), BF16),
+        (grad_out.shape[1:], BF16),
+        (w.shape, BF16),
+        (norm_gain.shape, F32),
         ((3, 27, 768), F32),
         ((4, 9, 8, 768), F32),
         ((8, 32, 128), BF16),
@@ -608,10 +631,11 @@
         kernel,
         out_shape=(jax.ShapeDtypeStruct(x.shape, BF16), jax.ShapeDtypeStruct(w.shape, F32),
                    jax.ShapeDtypeStruct(norm_gain.shape, F32)),
-        in_specs=[hbm] + [vmem] * 3,
+        in_specs=[hbm] * 4,
         out_specs=(hbm, vmem, vmem),
         scratch_shapes=[pltpu.VMEM(shape, kind) for shape, kind in scratch]
-        + [pltpu.SemaphoreType.DMA((26,)), pltpu.SemaphoreType.DMA((26,)), pltpu.SemaphoreType.DMA((2,))],
+        + [pltpu.SemaphoreType.DMA((26,)), pltpu.SemaphoreType.DMA((26,)), pltpu.SemaphoreType.DMA((5,)),
+           pltpu.SemaphoreType.REGULAR((3,))],
         compiler_params=pltpu.CompilerParams(collective_id=0, has_side_effects=True,
                                              vmem_limit_bytes=60 * 1024 * 1024),
     )(x, grad_out[0], w, norm_gain)

time: 77.4 us -> 77 us (level)
  no operation moved by 1% of the time
where the time goes in v5:
time: 77 us; the launch traced here: 76.8 us
  Pallas kernels  72.9 us (95%)
  local copies, waits for them, and re-layouts  3.26 us (4%)
    pallas_call x1, Pallas kernels, shards(): pl.pallas_call(kernel, out_shape=(jax.ShapeDtypeStruct(x.shape, BF16), ja...  72.9 us
    unnamed x7, local copies, waits for them, and re-layouts  3.26 us

profile of v5, /device:TPU:1, one launch (start us, length us, event | category | flops | bytes accessed | tf_op | source)
XLA Modules:
  0.0 76.8 jit_solution(10432123417080544042)
XLA Ops:
  0.6 72.9 %shard_map.67 = (bf16[48,8,768]{2,1,0:T(8,128)(2,1)}, f32[3,27,768]{2,1,0:T(8,128)}, f32[3,96]{1,0:T(4,128)}) custom-call(bf16[48,8,768]{2,1,0:T(8,128)(2,1)} %bitcast.13, bf16[2,2,4,768]{3,2,1,0:T(4,128)(2,1)} %bitcast.17, bf16[3,27,768]{2,1,0:T(8,128)(2,1)} %bitcast.16, f32[3,96]{1,0:T(4,128)} %gain_hbm.1), custom_call_target="tpu_custom_call" | custom-call | tf_op jit(solution)/shard_map/pallas_call | solution.py:630
  73.6 0.0 copy-start
  73.6 2.0 %copy.10 = bf16[1,4,4,8,3,768]{5,3,4,2,1,0:T(8,128)(2,1)} copy(bf16[1,4,4,8,3,768]{5,3,4,2,1,0:T(8,128)(2,1)} %bitcast.14) | data formatting | bytes 1179648
  75.5 0.0 copy-done
  75.5 0.0 copy-start.1
  75.5 0.7 copy.11
  76.2 0.0 copy-done.1
  76.3 0.6 copy.12
Async XLA Ops:
  73.6 2.0 %copy-start = (f32[3,27,768]{2,1,0:T(8,128)S(1)}, f32[3,27,768]{2,1,0:T(8,128)}, u32[]{:S(2)}) copy-start(f32[3,27,768]{2,1,0:T(8,128)} %get-tuple-element.7) | copy-start | bytes 746500
  75.5 0.7 copy-start.1

commit v6 on v5

--- a/solution.py
+++ b/solution.py
@@ -112,7 +112,7 @@
     barrier = pltpu.get_barrier_semaphore()
     greeted = [z_peer(k) for k in (4, 12, 3, 13, 2, 14, 1, 15)]
     greeted += [owner(d) for d in (17, 16, 1)] + [feeder(d) for d in (17, 16, 1)]
-    greeted += [seq_peer(1), seq_peer(-1)] + [quad_peer(k) for k in (3, 2, 1)] + [head_peer(k) for k in range(1, HEADS)]
+    greeted += [seq_peer(1), seq_peer(-1), seq_peer(1 + SEQ // 2), seq_peer(-1 - SEQ // 2)] + [quad_peer(k) for k in (3, 2, 1)] + [head_peer(k) for k in range(1, HEADS)]
     for peer in greeted:
         pl.semaphore_signal(barrier, inc=1, device_id=peer, device_id_type=MESH)
 
@@ -127,7 +127,7 @@
         for peer in peers:
             pl.semaphore_signal(ready.at[stage], inc=1, device_id=peer, device_id_type=MESH)
 
-    quad, four_on = [quad_peer(k) for k in (2, 3, 1)], [z_peer(4), z_peer(12)]
+    four_on = [z_peer(4), z_peer(12)]
     pending = []
 
     def drain():
@@ -208,14 +208,14 @@
     lax.fori_loop(0, 24, split_fine, 0)
 
     pl.semaphore_wait(barrier, len(greeted))
+    hand_on(0, four_on)
     for stage, src, dst in ((A2A_K, sbk, rbk), (A2A_Q, sbq, rbq)):
         for k in (4, 5, 3, 7, 1, 2, 6):
             peer = head_peer(k)
             send(stage, src.at[peer[1]], dst.at[k], peer)
         pending.append((stage, dst.at[pl.ds(1, HEADS - 1)]))
         dst[0] = src[n]
-    hand_on(0, quad)
-    pl.semaphore_wait(ready.at[0], 3)
+    pl.semaphore_wait(ready.at[0], 2)
     hand_on(1, four_on)
     arrived(A2A_K, rbk.at[pl.ds(1, HEADS - 1)])
 
@@ -255,8 +255,6 @@
 
     hs[0:128, :] = jnp.concatenate([pkv(0, 0), pkv(0, 1), pkv(1, 0), pkv(1, 1)], 0).astype(BF16)
     exchange((KV_OWN, KV_ROW, KV_FRAME, KV_CORNER), KV_SPANS, hs, hr, [owner(d) for d in (0, 1, 16, 17)])
-    pl.semaphore_wait(ready.at[1], 2)
-    hand_on(2, four_on)
     arrived(A2A_Q, rbq.at[pl.ds(1, HEADS - 1)])
     sets = [rbq[from_col[h]].astype(F32) for h in range(HEADS)]
     for grp in range(9):
@@ -268,7 +266,7 @@
                 v = v + jnp.where(row8 == 0, rolled[j - 1], 0.0)
             pe[grp * 32 + j * 8:grp * 32 + j * 8 + 8, :] = v
     hs[128:288, :] = jnp.concatenate([pq(0, 2), pq(1, 2), pq(2, 0), pq(2, 1), pq(2, 2)], 0).astype(BF16)
-    pl.semaphore_wait(ready.at[2], 2)
+    pl.semaphore_wait(ready.at[1], 2)
     exchange((Q_ROW, Q_FRAME, Q_CORNER), Q_SPANS, hs, hr, [seq_peer(d) for d in (1, 16, 17)])
     for k in range(1, HEADS):
         peer = head_peer(k)
@@ -635,7 +633,7 @@
         out_specs=(hbm, vmem, vmem),
         scratch_shapes=[pltpu.VMEM(shape, kind) for shape, kind in scratch]
         + [pltpu.SemaphoreType.DMA((26,)), pltpu.SemaphoreType.DMA((26,)), pltpu.SemaphoreType.DMA((5,)),
-           pltpu.SemaphoreType.REGULAR((3,))],
+           pltpu.SemaphoreType.REGULAR((2,))],
         compiler_params=pltpu.CompilerParams(collective_id=0, has_side_effects=True,
                                              vmem_limit_bytes=60 * 1024 * 1024),
     )(x, grad_out[0], w, norm_gain)

time: 77 us -> 75.9 us (0.986)
  Pallas kernels: 72.9 us -> 71.8 us
    pallas_call x1, Pallas kernels: 72.9 us -> 71.8 us  [shards(): pl.pallas_call(kernel, out_shape=(jax.ShapeDtypeStruct(x.shape, BF16), ja...]
where the time goes in v6:
time: 75.9 us; the launch traced here: 75.7 us
  Pallas kernels  71.8 us (95%)
  local copies, waits for them, and re-layouts  3.26 us (4%)
    pallas_call x1, Pallas kernels, shards(): pl.pallas_call(kernel, out_shape=(jax.ShapeDtypeStruct(x.shape, BF16), ja...  71.8 us
    unnamed x7, local copies, waits for them, and re-layouts  3.26 us

profile of v6, /device:TPU:1, one launch (start us, length us, event | category | flops | bytes accessed | tf_op | source)
XLA Modules:
  0.0 75.7 jit_solution(14587552871317329388)
XLA Ops:
  0.6 71.8 %shard_map.67 = (bf16[48,8,768]{2,1,0:T(8,128)(2,1)}, f32[3,27,768]{2,1,0:T(8,128)}, f32[3,96]{1,0:T(4,128)}) custom-call(bf16[48,8,768]{2,1,0:T(8,128)(2,1)} %bitcast.13, bf16[2,2,4,768]{3,2,1,0:T(4,128)(2,1)} %bitcast.17, bf16[3,27,768]{2,1,0:T(8,128)(2,1)} %bitcast.16, f32[3,96]{1,0:T(4,128)} %gain_hbm.1), custom_call_target="tpu_custom_call" | custom-call | tf_op jit(solution)/shard_map/pallas_call | solution.py:628
  72.5 0.0 copy-start
  72.5 2.0 %copy.10 = bf16[1,4,4,8,3,768]{5,3,4,2,1,0:T(8,128)(2,1)} copy(bf16[1,4,4,8,3,768]{5,3,4,2,1,0:T(8,128)(2,1)} %bitcast.14) | data formatting | bytes 1179648
  74.4 0.0 copy-done
  74.4 0.0 copy-start.1
  74.4 0.7 copy.11
  75.2 0.0 copy-done.1
  75.2 0.6 copy.12
Async XLA Ops:
  72.5 2.0 %copy-start = (f32[3,27,768]{2,1,0:T(8,128)S(1)}, f32[3,27,768]{2,1,0:T(8,128)}, u32[]{:S(2)}) copy-start(f32[3,27,768]{2,1,0:T(8,128)} %get-tuple-element.7) | copy-start | bytes 746500
  74.4 0.7 copy-start.1

commit v7 on v6

--- a/solution.py
+++ b/solution.py
@@ -110,9 +110,10 @@
 
 
     barrier = pltpu.get_barrier_semaphore()
-    greeted = [z_peer(k) for k in (4, 12, 3, 13, 2, 14, 1, 15)]
-    greeted += [owner(d) for d in (17, 16, 1)] + [feeder(d) for d in (17, 16, 1)]
-    greeted += [seq_peer(1), seq_peer(-1), seq_peer(1 + SEQ // 2), seq_peer(-1 - SEQ // 2)] + [quad_peer(k) for k in (3, 2, 1)] + [head_peer(k) for k in range(1, HEADS)]
+    greeted = [owner(17), feeder(17), owner(16), feeder(16), owner(1), feeder(1)]
+    greeted += [z_peer(k) for k in (4, 12, 3, 13)] + [head_peer(k) for k in (5, 3, 7, 1, 4)]
+    greeted += [z_peer(k) for k in (2, 14, 1, 15)] + [seq_peer(1), seq_peer(-1), seq_peer(1 + SEQ // 2), seq_peer(-1 - SEQ // 2)]
+    greeted += [head_peer(6), head_peer(2)] + [quad_peer(k) for k in (3, 2, 1)]
     for peer in greeted:
         pl.semaphore_signal(barrier, inc=1, device_id=peer, device_id_type=MESH)
 
@@ -210,7 +211,7 @@
     pl.semaphore_wait(barrier, len(greeted))
     hand_on(0, four_on)
     for stage, src, dst in ((A2A_K, sbk, rbk), (A2A_Q, sbq, rbq)):
-        for k in (4, 5, 3, 7, 1, 2, 6):
+        for k in (5, 3, 7, 1, 4, 6, 2):
             peer = head_peer(k)
             send(stage, src.at[peer[1]], dst.at[k], peer)
         pending.append((stage, dst.at[pl.ds(1, HEADS - 1)]))
@@ -245,7 +246,7 @@
         return jnp.concatenate([pe[at:at + 16, :], pe[at + 64:at + 80, :]], 0)
 
     def exchange(stages, spans, src, dst, peers):
-        for stage, (lo, count), peer in zip(stages, spans, peers):
+        for stage, (lo, count), peer in list(zip(stages, spans, peers))[::-1]:
             send(stage, src.at[pl.ds(lo, count)], dst.at[pl.ds(lo, count)], peer)
             pending.append((stage, dst.at[pl.ds(lo, count)]))
 

time: 75.9 us -> 75.7 us (level)
  no operation moved by 1% of the time
where the time goes in v7:
time: 75.7 us; the launch traced here: 75.5 us
  Pallas kernels  71.6 us (95%)
  local copies, waits for them, and re-layouts  3.26 us (4%)
    pallas_call x1, Pallas kernels, shards(): pl.pallas_call(kernel, out_shape=(jax.ShapeDtypeStruct(x.shape, BF16), ja...  71.6 us
    unnamed x7, local copies, waits for them, and re-layouts  3.26 us

profile of v7, /device:TPU:1, one launch (start us, length us, event | category | flops | bytes accessed | tf_op | source)
XLA Modules:
  0.0 75.5 jit_solution(8674930007832408494)
XLA Ops:
  0.6 71.6 %shard_map.67 = (bf16[48,8,768]{2,1,0:T(8,128)(2,1)}, f32[3,27,768]{2,1,0:T(8,128)}, f32[3,96]{1,0:T(4,128)}) custom-call(bf16[48,8,768]{2,1,0:T(8,128)(2,1)} %bitcast.13, bf16[2,2,4,768]{3,2,1,0:T(4,128)(2,1)} %bitcast.17, bf16[3,27,768]{2,1,0:T(8,128)(2,1)} %bitcast.16, f32[3,96]{1,0:T(4,128)} %gain_hbm.1), custom_call_target="tpu_custom_call" | custom-call | tf_op jit(solution)/shard_map/pallas_call | solution.py:629
  72.3 0.0 copy-start
  72.3 2.0 %copy.10 = bf16[1,4,4,8,3,768]{5,3,4,2,1,0:T(8,128)(2,1)} copy(bf16[1,4,4,8,3,768]{5,3,4,2,1,0:T(8,128)(2,1)} %bitcast.14) | data formatting | bytes 1179648
  74.2 0.0 copy-done
  74.2 0.0 copy-start.1
  74.2 0.7 copy.11
  75.0 0.0 copy-done.1
  75.0 0.6 copy.12
Async XLA Ops:
  72.3 2.0 %copy-start = (f32[3,27,768]{2,1,0:T(8,128)S(1)}, f32[3,27,768]{2,1,0:T(8,128)}, u32[]{:S(2)}) copy-start(f32[3,27,768]{2,1,0:T(8,128)} %get-tuple-element.7) | copy-start | bytes 746500
  74.2 0.7 copy-start.1

commit v8 on v6

--- a/solution.py
+++ b/solution.py
@@ -512,6 +512,15 @@
         send(SUM_Z, zs.at[0], zs.at[k], z_peer(k))
     pending.append((SUM_Z, zs.at[pl.ds(1, ZS - 1)]))
 
+    arrived(SUM_Z, zs.at[pl.ds(1, ZS - 1)])
+    v = zs[z].astype(F32)
+    for k in range(1, ZS):
+        v = v + zs[lax.rem(z - k + ZS, ZS)].astype(F32)
+    fr[0] = v.astype(BF16)
+    for p in range(31, 0, -1):
+        send(SPREAD, fr.at[0], fr.at[p], plane_peer(p))
+    pending.append((SPREAD, fr.at[pl.ds(1, 31)]))
+
     arrived(A2A_B, rb2.at[pl.ds(1, HEADS - 1)])
     tiles = merge_heads([rb2[from_col[h]].astype(F32) for h in range(HEADS)])
     for j in range(6):
@@ -545,14 +554,6 @@
     store = pltpu.make_async_copy(gxv, gx_ref, local.at[4])
     store.start()
 
-    arrived(SUM_Z, zs.at[pl.ds(1, ZS - 1)])
-    v = zs[z].astype(F32)
-    for k in range(1, ZS):
-        v = v + zs[lax.rem(z - k + ZS, ZS)].astype(F32)
-    fr[0] = v.astype(BF16)
-    for p in range(31, 0, -1):
-        send(SPREAD, fr.at[0], fr.at[p], plane_peer(p))
-    pending.append((SPREAD, fr.at[pl.ds(1, 31)]))
     arrived(SPREAD, fr.at[pl.ds(1, 31)])
 
     lane16 = iota((16, 128), 1)

time: 75.9 us -> 75.9 us (level)
  no operation moved by 1% of the time
where the time goes in v8:
time: 75.9 us; the launch traced here: 75.7 us
  Pallas kernels  71.8 us (95%)
  local copies, waits for them, and re-layouts  3.26 us (4%)
    pallas_call x1, Pallas kernels, shards(): pl.pallas_call(kernel, out_shape=(jax.ShapeDtypeStruct(x.shape, BF16), ja...  71.8 us
    unnamed x7, local copies, waits for them, and re-layouts  3.26 us

profile of v8, /device:TPU:1, one launch (start us, length us, event | category | flops | bytes accessed | tf_op | source)
XLA Modules:
  0.0 75.7 jit_solution(13659729277339136889)
XLA Ops:
  0.6 71.8 %shard_map.67 = (bf16[48,8,768]{2,1,0:T(8,128)(2,1)}, f32[3,27,768]{2,1,0:T(8,128)}, f32[3,96]{1,0:T(4,128)}) custom-call(bf16[48,8,768]{2,1,0:T(8,128)(2,1)} %bitcast.13, bf16[2,2,4,768]{3,2,1,0:T(4,128)(2,1)} %bitcast.17, bf16[3,27,768]{2,1,0:T(8,128)(2,1)} %bitcast.16, f32[3,96]{1,0:T(4,128)} %gain_hbm.1), custom_call_target="tpu_custom_call" | custom-call | tf_op jit(solution)/shard_map/pallas_call | solution.py:629
  72.5 0.0 copy-start
  72.5 2.0 %copy.10 = bf16[1,4,4,8,3,768]{5,3,4,2,1,0:T(8,128)(2,1)} copy(bf16[1,4,4,8,3,768]{5,3,4,2,1,0:T(8,128)(2,1)} %bitcast.14) | data formatting | bytes 1179648
  74.4 0.0 copy-done
  74.4 0.0 copy-start.1
  74.4 0.7 copy.11
  75.2 0.0 copy-done.1
  75.2 0.6 copy.12
Async XLA Ops:
  72.5 2.0 %copy-start = (f32[3,27,768]{2,1,0:T(8,128)S(1)}, f32[3,27,768]{2,1,0:T(8,128)}, u32[]{:S(2)}) copy-start(f32[3,27,768]{2,1,0:T(8,128)} %get-tuple-element.7) | copy-start | bytes 746500
  74.4 0.7 copy-start.1
